TPU v7x, 32 devices: a whole 2x2x4 slice. The times are simulated.
32 devices in a mesh: dp: 4 (over y, x), vocab: 8 (over z, core).
Axes of the slice: x: 2, y: 2, z: 4, core: 2. Of those that a mesh axis runs over, the one named last changes fastest.
Arguments:
- hidden: bfloat16 [256, 4096], P(('dp', 'vocab')), may hold values from -250 to 250
- targets: int32 [256], P(('dp', 'vocab')), may hold values from 0 to 71679, as said below
- loss_weight: bfloat16 [256], P(('dp', 'vocab')), may hold values from 0.5 to 2
- head_weight: bfloat16 [4096, 10240], P(None, 'vocab'), may hold values from -0.09375 to 0.09375
- cluster_weight: bfloat16 [4096, 8], P(None, 'vocab'), may hold values from -0.09375 to 0.09375
- tail_proj: bfloat16 [8, 4096, 1024], P('vocab', None, 'dp'), may hold values from -0.09375 to 0.09375
- tail_out: bfloat16 [8, 1024, 7680], P('vocab', 'dp'), may hold values from -0.1875 to 0.1875
Outputs:
- hidden_grad: bfloat16 [256, 4096], P(('dp', 'vocab'))
- head_grad: bfloat16 [4096, 10240], P('dp', 'vocab')
- cluster_grad: bfloat16 [4096, 8], P('dp', 'vocab')
- proj_grad: bfloat16 [8, 4096, 1024], P('vocab', None, 'dp')
- out_grad: bfloat16 [8, 1024, 7680], P('vocab', 'dp')
Inputs may be any that keep to these rules, and one draw needn't show every extreme that they name: In each block of 64 consecutive tokens exactly 32 targets are at or above 10240; at most 16 of them fall in one cluster, and some cluster holds exactly 16 of them in every block.
All inputs are finite; a program needn't handle non-finite values.
Results may differ from a plain program's by a relative error of at most 0.012.
The roundings to bfloat16 on the way count: a program that leaves them out, or rounds other values in their place, can miss the bound.
Values may be sent and summed in bfloat16 or wider, within the bound.
A program may use at most 128 MiB of HBM per device.

v0:
```python
import jax
import jax.numpy as jnp
from jax import lax
from jax.sharding import PartitionSpec as P

HEAD = 10240
CV = 7680
CLUSTER_TOKEN_CAP = 16


def combined_all(part, axis, combine):
    gathered = jax.tree.map(lambda a: lax.all_gather(a, axis), part)

    def take(source):
        return jax.tree.map(lambda a: lax.dynamic_index_in_dim(a, source, 0, False), gathered)

    return lax.fori_loop(
        1, lax.axis_size(axis), lambda source, state: combine(state, take(source)), take(0)
    )


def merge_soft(first, second):
    top = jnp.maximum(first[0], second[0])
    total = first[1] * jnp.exp(first[0] - top) + second[1] * jnp.exp(second[0] - top)
    return (top, total)


def pick_rows(hidden_block_list, target_blocks, weight_blocks, cluster):
    offset = target_blocks - HEAD
    member = (offset >= 0) & (offset // CV == cluster)
    rank = jnp.cumsum(member.astype(jnp.int32), axis=1) - 1
    slots = jnp.arange(CLUSTER_TOKEN_CAP, dtype=jnp.int32)
    select = member[:, None, :] & (rank[:, None, :] == slots[None, :, None])
    cluster_selector = select.astype(jnp.bfloat16)
    token_row_list = jnp.einsum(
        "ahw,awo->aho", cluster_selector, hidden_block_list, preferred_element_type=jnp.float32
    ).astype(jnp.bfloat16)
    words = jnp.sum(jnp.where(select, (offset % CV)[:, None, :], 0), axis=2).astype(jnp.int32)
    gains = jnp.sum(
        jnp.where(select, weight_blocks.astype(jnp.float32)[:, None, :], 0.0), axis=2
    ).astype(jnp.bfloat16)
    return (token_row_list, words, gains, select)


def shards(hidden, targets, loss_weight, head_weight, cluster_weight, tail_proj, tail_out):
    vocab_index = lax.axis_index("vocab")
    rows_hidden, row_targets, row_weights = (
        lax.all_gather(hidden, "vocab", axis=0, tiled=True),
        lax.all_gather(targets, "vocab", axis=0, tiled=True),
        lax.all_gather(loss_weight, "vocab", axis=0, tiled=True),
    )
    picked, own_words, own_gains, select = pick_rows(
        rows_hidden[None], row_targets[None], row_weights[None], vocab_index
    )
    own_select = select[0]
    tail_rows, words, gains = (
        lax.all_gather(picked[0], "dp", axis=0, tiled=True),
        lax.all_gather(own_words[0], "dp", axis=0, tiled=True),
        lax.all_gather(own_gains[0], "dp", axis=0, tiled=True),
    )
    gain_rows = row_weights.astype(jnp.float32)
    local_logits = jnp.dot(rows_hidden, head_weight, preferred_element_type=jnp.float32)
    cluster_logit = jnp.dot(rows_hidden, cluster_weight, preferred_element_type=jnp.float32)
    width = head_weight.shape[1]
    columns = vocab_index * width + jnp.arange(width, dtype=jnp.int32)
    offset = row_targets - HEAD
    target_column = jnp.where(offset >= 0, HEAD + offset // CV, row_targets).astype(jnp.int32)
    top = jnp.maximum(jnp.max(local_logits, axis=1), cluster_logit[:, 0])
    total = jnp.sum(jnp.exp(local_logits - top[:, None]), axis=1) + jnp.exp(
        cluster_logit[:, 0] - top
    )
    top, total = combined_all((top, total), "vocab", merge_soft)
    head_hot = (columns[None, :] == target_column[:, None]).astype(jnp.float32)
    head_delta = (
        gain_rows[:, None] * (jnp.exp(local_logits - top[:, None]) / total[:, None] - head_hot)
    ).astype(jnp.bfloat16)
    cluster_hot = (target_column == HEAD + vocab_index).astype(jnp.float32)[:, None]
    cluster_delta = (
        gain_rows[:, None] * (jnp.exp(cluster_logit - top[:, None]) / total[:, None] - cluster_hot)
    ).astype(jnp.bfloat16)
    head_partial = lax.dot_general(
        rows_hidden, head_delta, (((0,), (0,)), ((), ())), preferred_element_type=jnp.float32
    )
    cluster_partial = lax.dot_general(
        rows_hidden, cluster_delta, (((0,), (0,)), ((), ())), preferred_element_type=jnp.float32
    )
    token_partial = lax.dot_general(
        head_delta, head_weight, (((1,), (1,)), ((), ())), preferred_element_type=jnp.float32
    )
    token_partial = token_partial + lax.dot_general(
        cluster_delta, cluster_weight, (((1,), (1,)), ((), ())), preferred_element_type=jnp.float32
    )
    proj = tail_proj[0]
    out = tail_out[0]
    gain_tail = gains.astype(jnp.float32)
    reduced = jnp.dot(tail_rows, proj, preferred_element_type=jnp.float32).astype(jnp.bfloat16)
    partial_logits = jnp.dot(reduced, out, preferred_element_type=jnp.float32)
    word_logits = lax.psum(partial_logits, "dp")
    word_top = jnp.max(word_logits, axis=1, keepdims=True)
    word_exp = jnp.exp(word_logits - word_top)
    word_prob = word_exp / jnp.sum(word_exp, axis=1, keepdims=True)
    word_columns = jnp.arange(word_logits.shape[1], dtype=jnp.int32)
    word_hot = (word_columns[None, :] == words[:, None]).astype(jnp.float32)
    word_delta = (gain_tail[:, None] * (word_prob - word_hot)).astype(jnp.bfloat16)
    reduced_grad = lax.dot_general(
        word_delta, out, (((1,), (1,)), ((), ())), preferred_element_type=jnp.float32
    ).astype(jnp.bfloat16)
    out_grad = lax.dot_general(
        reduced, word_delta, (((0,), (0,)), ((), ())), preferred_element_type=jnp.float32
    ).astype(jnp.bfloat16)
    proj_grad = lax.dot_general(
        tail_rows, reduced_grad, (((0,), (0,)), ((), ())), preferred_element_type=jnp.float32
    ).astype(jnp.bfloat16)
    tail_partial = lax.dot_general(
        reduced_grad, proj, (((1,), (1,)), ((), ())), preferred_element_type=jnp.float32
    )
    head_sum, cluster_sum, tail_sum = (
        lax.psum_scatter(
            head_partial.astype(jnp.bfloat16), "dp", scatter_dimension=0, tiled=True
        ).astype(jnp.float32),
        lax.psum_scatter(
            cluster_partial.astype(jnp.bfloat16), "dp", scatter_dimension=0, tiled=True
        ).astype(jnp.float32),
        lax.psum_scatter(
            tail_partial.astype(jnp.bfloat16), "dp", scatter_dimension=0, tiled=True
        ).astype(jnp.float32),
    )
    spread_back = jnp.dot(
        own_select.astype(jnp.float32).T, tail_sum, precision=lax.Precision.HIGHEST
    )
    token_partial = token_partial + spread_back
    hidden_grad = lax.psum_scatter(token_partial, "vocab", scatter_dimension=0, tiled=True).astype(
        jnp.bfloat16
    )
    return (
        hidden_grad,
        head_sum.astype(jnp.bfloat16),
        cluster_sum.astype(jnp.bfloat16),
        proj_grad[None],
        out_grad[None],
    )


def solution(mesh):
    placed = (
        P(("dp", "vocab"), None),
        P(("dp", "vocab")),
        P(("dp", "vocab")),
        P(None, "vocab"),
        P(None, "vocab"),
        P("vocab", None, "dp"),
        P("vocab", "dp", None),
    )
    return jax.shard_map(
        shards,
        mesh=mesh,
        in_specs=placed,
        out_specs=(
            P(("dp", "vocab"), None),
            P("dp", "vocab"),
            P("dp", "vocab"),
            P("vocab", None, "dp"),
            P("vocab", "dp", None),
        ),
        check_vma=False,
    )
```

profile of v0, /device:TPU:0, one launch (start us, length us, event | category | flops | bytes accessed | tf_op | source)
XLA Modules:
  0.0 331.6 jit_solution(12851226901862909016)
XLA Ops:
  7.2 16.9 %all_gather.31 = bf16[64,4096]{1,0:T(8,128)(2,1)S(1)} all-gather(bf16[8,4096]{1,0:T(8,128)(2,1)} %param.9), channel_id=1, replica_groups=mesh['dp'=4,'vocab'=8] {'vocab'}, dimensions={0}, use_global_device_ids=true | all-gather | bytes 589824 | tf_op jit(solution)/shard_map/all_gather | solution.py:48
  24.2 1.2 dynamic-slice
  26.1 0.9 dynamic-update-slice.3
  26.9 8.9 %all-reduce.3 = s32[64]{0:T(128)S(1)} all-reduce(s32[64]{0:T(128)S(1)} %dynamic-update-slice.3), channel_id=1, replica_groups=mesh['dp'=4,'vocab'=8] {'vocab'}, use_global_device_ids=true, to_apply=%add.3 | all-reduce | flops 64 | bytes 512
  36.4 10.6 %all_gather.38 = bf16[64,4096]{1,0:T(8,128)(2,1)S(1)} all-gather(bf16[16,4096]{1,0:T(8,128)(2,1)S(1)} %convolution_convert_fusion.4), channel_id=1, replica_groups=mesh['dp'=4,'vocab'=8] {'dp'}, dimensions={0}, use_global_device_ids=true | all-gather | bytes 655360 | tf_op jit(solution)/shard_map/all_gather | solution.py:57
  47.4 2.1 fusion.7
  50.5 6.7 %fusion.35 = (f32[64]{0:T(128)S(1)}, f32[64,1280]{1,0:T(8,128)S(1)}) fusion(bf16[64,4096]{1,0:T(8,128)(2,1)S(1)} %all_gather.31, bf16[4096,1280]{1,0:T(8,128)(2,1)} %param.12), kind=kOutput, calls=%fused_computation.60 | convolution fusion | flops 671170496 | bytes 11337984 | tf_op jit(solution)/shard_map/dot_general | solution.py:62
  58.3 13.6 %all-reduce.6 = (f32[512]{0:T(512)S(1)}, f32[512]{0:T(512)S(1)}) all-reduce(f32[512]{0:T(512)S(1)} %get-tuple-element.180, f32[512]{0:T(512)S(1)} %add_dynamic-update-slice_fusion), channel_id=2, replica_groups=mesh['dp'=4,'vocab'=8] {'vocab'}, use_global_device_ids=true, to_apply=%add.1 | all-reduce | flops 1024 | bytes 8192
  72.2 13.6 %all-reduce = bf16[64]{0:T(256)(128)(2,1)S(1)} all-reduce(bf16[64]{0:T(256)(128)(2,1)S(1)} %dynamic-update-slice), channel_id=1, replica_groups=mesh['dp'=4,'vocab'=8] {'vocab'}, use_global_device_ids=true, to_apply=%add | all-reduce | flops 64 | bytes 256
  85.8 1.2 dynamic-slice.4
  89.0 9.3 %all-reduce.4 = bf16[64]{0:T(256)(128)(2,1)S(1)} all-reduce(bf16[64]{0:T(256)(128)(2,1)S(1)} %dynamic-update-slice.4), channel_id=1, replica_groups=mesh['dp'=4,'vocab'=8] {'dp'}, use_global_device_ids=true, to_apply=%add.4 | all-reduce | flops 64 | bytes 256
  99.2 7.8 %all-reduce.5 = s32[64]{0:T(128)} all-reduce(s32[64]{0:T(128)S(1)} %dynamic-update-slice.5), channel_id=1, replica_groups=mesh['dp'=4,'vocab'=8] {'dp'}, use_global_device_ids=true, to_apply=%add.5 | all-reduce | flops 64 | bytes 512
  107.0 8.5 %all-reduce.9.cloned.1.call-done = f32[64,7680]{1,0:T(8,128)} async-done(((f32[64,7680]{1,0:T(8,128)}), f32[64,7680]{1,0:T(8,128)}) %all-reduce.9.cloned.1.call-update) | async-done | bytes 1966096 | tf_op jit(solution)/shard_map/psum | solution.py:98
  115.5 1.7 reduce_max.19
  117.3 2.1 fusion.12
  119.4 3.5 %fusion.13 = bf16[64,256]{1,0:T(8,128)(2,1)S(1)} fusion(bf16[1,256,7680]{2,1,0:T(8,128)(2,1)} %param.15, f32[64,7680]{1,0:T(8,128)S(1)} %copy-done.1, s32[64]{0:T(128)S(1)} %copy-done.14, f32[64]{0:T(128)S(1)} %fusion.12, f32[64]{0:T(128)S(1)} %reduce_max.19, f32[64]{0:T(128)} %convert_element_type.82), kind=kOutput, calls=%fused_computation.27 | convolution fusion | flops 255115264 | bytes 5932032 | tf_op jit(solution)/shard_map/dot_general | solution.py:105
  122.9 1.6 convolution_convert_fusion.3
  124.7 1.6 reshape.345
  126.4 1.4 reduce.2
  127.8 0.7 convert.10
  128.5 8.3 %convolution_add_fusion.1 = f32[64,4096]{1,0:T(8,128)} fusion(bf16[4096,1280]{1,0:T(8,128)(2,1)} %param.12, f32[4096]{0:T(1024)S(1)} %convert.10, f32[64]{0:T(128)} %get-tuple-element.177, f32[64,1280]{1,0:T(8,128)S(1)} %get-tuple-element.184, s32[1280]{0:T(1024)S(1)} %iota_add_fusion, f32[64]{0:T(128)S(1)} %get-tuple-element.139, ...), kind=kOutput, calls=%fused_computation.13 | convolution fusion | flops 672186368 | bytes 11884800 | tf_op jit(solution)/shard_map/dot_general | solution.py:87
  136.8 12.6 %reduce-scatter.7.cloned.1.call-done = bf16[16,4096]{1,0:T(8,128)(2,1)} async-done(((bf16[64,4096]{1,0:T(8,128)(2,1)}), bf16[16,4096]{1,0:T(8,128)(2,1)}) %reduce-scatter.7.cloned.1.call-update) | async-done | bytes 131088 | tf_op jit(solution)/shard_map/reduce_scatter | solution.py:124
  149.4 2.6 convolution_add_fusion
  152.3 6.3 %fusion.2 = bf16[4096,1280]{0,1:T(8,128)(2,1)} fusion(bf16[64,4096]{1,0:T(8,128)(2,1)S(1)} %all_gather.31, f32[64,1280]{1,0:T(8,128)S(1)} %get-tuple-element.184, s32[1280]{0:T(1024)S(1)} %iota_add_fusion, f32[64]{0:T(128)S(1)} %get-tuple-element.139, f32[64]{0:T(128)S(1)} %get-tuple-element.138, f32[64]{0:T(128)} %copy-done.5, s32[64]{0:T(128)} %get-tuple-element.179), kind=kOutput, calls=%fused_computation.7 | convolution fusion | flops 676904960 | bytes 11343872 | tf_op jit(solution)/shard_map/dot_general | solution.py:81
  158.7 22.2 %reduce-scatter.13.cloned.1.call-done = bf16[1024,1]{1,0:T(8,128)(2,1)} async-done(((bf16[4096,1]{1,0:T(8,128)(2,1)}), bf16[1024,1]{1,0:T(8,128)(2,1)}) %reduce-scatter.13.cloned.1.call-update) | async-done | bytes 2064
  180.9 1.7 copy.21
  182.5 2.1 fusion.4
  184.6 3.2 fusion.3
  187.8 27.9 %reduce-scatter.9.cloned.1.call-done = f32[8,4096]{1,0:T(8,128)} async-done(((f32[64,4096]{1,0:T(8,128)}), f32[8,4096]{1,0:T(8,128)}) %reduce-scatter.9.cloned.1.call-update) | async-done | bytes 131088 | tf_op jit(solution)/shard_map/reduce_scatter | solution.py:132
  215.8 1.5 convert_element_type.89
  217.3 103.4 %reduce-scatter.11.cloned.1.call-done = bf16[1024,1280]{0,1:T(8,128)(2,1)} async-done(((bf16[4096,1280]{0,1:T(8,128)(2,1)}), bf16[1024,1280]{0,1:T(8,128)(2,1)}) %reduce-scatter.11.cloned.1.call-update) | async-done | bytes 2621456 | tf_op jit(solution)/shard_map/reduce_scatter | solution.py:118
  320.7 4.4 %copy.19 = bf16[1024,1280]{1,0:T(8,128)(2,1)} copy(bf16[1024,1280]{0,1:T(8,128)(2,1)} %reduce-scatter.11.cloned.1.call-done) | data formatting | bytes 5242880
  (81 shorter events, 5.7 us)
Async XLA Ops:
  7.2 39.8 %copy-start = (bf16[1,4096,256]{2,1,0:T(8,128)(2,1)S(1)}, bf16[1,4096,256]{2,1,0:T(8,128)(2,1)}, u32[]{:S(2)}) copy-start(bf16[1,4096,256]{2,1,0:T(8,128)(2,1)} %param.14) | copy-start | bytes 6291460
  7.2 108.3 %all-reduce.9.cloned.1.call-start = ((), (), s32[]{:S(2)}) async-start(), calls=%async_computation.4 | async-start | bytes 3932160 | tf_op jit(solution)/shard_map/psum | solution.py:98
  35.9 63.0 %copy-start.7 = (pred[64]{0:T(512)(128)(4,1)}, pred[64]{0:T(512)(128)(4,1)S(1)}, u32[]{:S(2)}) copy-start(pred[64]{0:T(512)(128)(4,1)S(1)} %get-tuple-element.175) | copy-start | bytes 196
  36.2 62.7 %copy-start.6 = (s32[64]{0:T(128)}, s32[64]{0:T(128)S(1)}, u32[]{:S(2)}) copy-start(s32[64]{0:T(128)S(1)} %add_reduce_fusion) | copy-start | bytes 772
  36.2 11.2 %copy-start.3 = (bf16[1,256,7680]{2,1,0:T(8,128)(2,1)S(1)}, bf16[1,256,7680]{2,1,0:T(8,128)(2,1)}, u32[]{:S(2)}) copy-start(bf16[1,256,7680]{2,1,0:T(8,128)(2,1)} %param.15) | copy-start | bytes 11796484
  49.5 0.7 copy-start.4
  49.5 99.8 %reduce-scatter.7.cloned.1.call-start = ((), (), s32[]{:S(2)}) async-start(), calls=%async_computation.5 | async-start | bytes 655360 | tf_op jit(solution)/shard_map/reduce_scatter | solution.py:124
  50.5 21.5 %copy-start.12 = (bf16[8]{0:T(256)(128)(2,1)S(1)}, bf16[8]{0:T(256)(128)(2,1)}, u32[]{:S(2)}) copy-start(bf16[8]{0:T(256)(128)(2,1)} %param.11) | copy-start | bytes 52
  88.6 28.6 %copy-start.5 = (f32[64]{0:T(128)}, f32[64]{0:T(128)S(1)}, u32[]{:S(2)}) copy-start(f32[64]{0:T(128)S(1)} %get-tuple-element.182) | copy-start | bytes 772
  117.3 5.6 %copy-start.8 = (f32[64]{0:T(128)}, f32[64]{0:T(128)S(1)}, u32[]{:S(2)}) copy-start(f32[64]{0:T(128)S(1)} %reduce_max.19) | copy-start | bytes 772
  117.3 2.1 copy-start.1
  117.3 2.1 copy-start.14
  119.4 3.5 %copy-start.10 = (f32[64]{0:T(128)}, f32[64]{0:T(128)S(1)}, u32[]{:S(2)}) copy-start(f32[64]{0:T(128)S(1)} %fusion.12) | copy-start | bytes 772
  124.5 56.4 %reduce-scatter.13.cloned.1.call-start = ((), (), s32[]{:S(2)}) async-start(), calls=%async_computation.8 | async-start | bytes 1310720
  126.3 89.5 %reduce-scatter.9.cloned.1.call-start = ((), (), s32[]{:S(2)}) async-start(), calls=%async_computation.6 | async-start | bytes 1179648 | tf_op jit(solution)/shard_map/reduce_scatter | solution.py:132
  152.0 168.7 %reduce-scatter.11.cloned.1.call-start = ((), (), s32[]{:S(2)}) async-start(), calls=%async_computation.7 | async-start | bytes 13107200 | tf_op jit(solution)/shard_map/reduce_scatter | solution.py:118
  158.6 26.0 %copy-start.9 = (f32[64]{0:T(128)S(1)}, f32[64]{0:T(128)}, u32[]{:S(2)}) copy-start(f32[64]{0:T(128)} %copy-done.8) | copy-start | bytes 772
  158.6 26.0 %copy-start.11 = (f32[64]{0:T(128)S(1)}, f32[64]{0:T(128)}, u32[]{:S(2)}) copy-start(f32[64]{0:T(128)} %copy-done.10) | copy-start | bytes 772
  158.6 26.0 %copy-start.13 = (f32[64]{0:T(128)S(1)}, f32[64]{0:T(128)}, u32[]{:S(2)}) copy-start(f32[64]{0:T(128)} %convert_element_type.82) | copy-start | bytes 772
  158.6 26.0 %copy-start.15 = (s32[64]{0:T(128)S(1)}, s32[64]{0:T(128)}, u32[]{:S(2)}) copy-start(s32[64]{0:T(128)} %all-reduce.5) | copy-start | bytes 772
  182.5 2.1 copy-start.2
Sparse Core Ops, SparseCore 0:
  49.7 65.7 all-reduce.8
  124.6 24.7 reduce-scatter.6
  153.1 27.7 reduce-scatter.12
  183.6 32.1 reduce-scatter.8
  218.7 101.9 reduce-scatter.10
where the time goes:
time: 332 us
  waiting for transfers between devices  175 us (53%)
  blocking collectives  80.7 us (24%)
  matrix products  37.4 us (11%)
  between operations  16 us (5%)
  local copies, waits for them, and re-layouts  12.7 us (4%)
  other arithmetic  9.65 us (3%)
    reduce_scatter x1, waiting for transfers between devices, shards(): lax.psum_scatter(head_partial.astype(jnp.bfloat16), 'dp', scatter_dimensi...  103 us
    unnamed x5, blocking collectives  53.2 us
    reduce_scatter x1, waiting for transfers between devices, shards(): lax.psum_scatter(token_partial, 'vocab', scatter_dimension=0, tiled=True)  27.9 us
    unnamed x6, waiting for transfers between devices  22.3 us
    all_gather x1, blocking collectives, shards(): lax.all_gather(hidden, 'vocab', axis=0, tiled=True)  16.9 us
    reduce_scatter x1, waiting for transfers between devices, shards(): lax.psum_scatter(tail_partial.astype(jnp.bfloat16), 'dp', scatter_dimensi...  12.6 us
    unnamed x46, local copies, waits for them, and re-layouts  10.8 us
    all_gather x1, blocking collectives, shards(): lax.all_gather(picked[0], 'dp', axis=0, tiled=True)  10.6 us
  transfers between devices with their start and end apart: 5, of which 5 were waited for; matrix products, arithmetic and copies ran while one was open for 12% of the time, Pallas kernels for 0%

commit v1 on v0

v1 whole, which is shorter than its diff:
```python
import jax
import jax.numpy as jnp
from jax import lax
from jax.sharding import PartitionSpec as P

HEAD = 10240
CV = 7680
CLUSTER_TOKEN_CAP = 16


def shards(hidden, targets, loss_weight, head_weight, cluster_weight, tail_proj, tail_out):
    vocab_index = lax.axis_index("vocab")
    dp_index = lax.axis_index("dp")
    n_dp = lax.axis_size("dp")
    n_vocab = lax.axis_size("vocab")
    local, model = hidden.shape
    span = local * n_vocab
    share = model // n_dp
    cap = CLUSTER_TOKEN_CAP
    f32, bf16 = jnp.float32, jnp.bfloat16

    facts = lax.all_gather(
        jnp.stack([targets.astype(f32), loss_weight.astype(f32)]),
        ("dp", "vocab"), axis=1, tiled=True,
    )
    all_targets = facts[0].astype(jnp.int32)
    all_weights = facts[1]
    all_hidden = lax.all_gather(hidden, ("dp", "vocab"), axis=0, tiled=True)
    rows_hidden = lax.dynamic_slice_in_dim(all_hidden, dp_index * span, span, 0)
    row_targets = lax.dynamic_slice_in_dim(all_targets, dp_index * span, span, 0)
    gain_rows = lax.dynamic_slice_in_dim(all_weights, dp_index * span, span, 0)

    blocks = all_targets.reshape(n_dp, span)
    offset = blocks - HEAD
    member = (offset >= 0) & (offset // CV == vocab_index)
    place = jnp.arange(span, dtype=jnp.int32)
    rank = jnp.sum(
        (member[:, None, :] & (place[None, None, :] < place[None, :, None])).astype(jnp.int32), axis=2
    )
    slots = jnp.arange(cap, dtype=jnp.int32)
    select = member[:, None, :] & (rank[:, None, :] == slots[None, :, None])
    own_select = lax.dynamic_index_in_dim(select, dp_index, 0, False)
    own_words = jnp.sum(
        jnp.where(own_select, (row_targets - HEAD)[None, :] % CV, 0), axis=1
    ).astype(jnp.int32)
    own_gains = jnp.sum(jnp.where(own_select, gain_rows[None, :], 0.0), axis=1)
    tail_rows = jnp.einsum(
        "ahw,awo->aho", select.astype(bf16), all_hidden.reshape(n_dp, span, model),
        preferred_element_type=f32,
    ).astype(bf16).reshape(n_dp * cap, model)

    proj = tail_proj[0]
    out = tail_out[0]
    reduced = jnp.dot(tail_rows, proj, preferred_element_type=f32).astype(bf16)
    partial_logits = jnp.dot(reduced, out, preferred_element_type=f32)
    word_logits = lax.psum_scatter(partial_logits, "dp", scatter_dimension=0, tiled=True)

    local_logits = jnp.dot(rows_hidden, head_weight, preferred_element_type=f32)
    cluster_logit = jnp.dot(rows_hidden, cluster_weight, preferred_element_type=f32)
    width = head_weight.shape[1]
    columns = vocab_index * width + jnp.arange(width, dtype=jnp.int32)
    row_offset = row_targets - HEAD
    target_column = jnp.where(row_offset >= 0, HEAD + row_offset // CV, row_targets)
    top = jnp.maximum(jnp.max(local_logits, axis=1), cluster_logit[:, 0])
    total = jnp.sum(jnp.exp(local_logits - top[:, None]), axis=1) + jnp.exp(cluster_logit[:, 0] - top)
    stats = lax.all_gather(jnp.stack([top, total]), "vocab")
    top = jnp.max(stats[:, 0], axis=0)
    total = jnp.sum(stats[:, 1] * jnp.exp(stats[:, 0] - top[None, :]), axis=0)
    head_hot = (columns[None, :] == target_column[:, None]).astype(f32)
    head_delta = (
        gain_rows[:, None] * (jnp.exp(local_logits - top[:, None]) / total[:, None] - head_hot)
    ).astype(bf16)
    cluster_hot = (target_column == HEAD + vocab_index).astype(f32)[:, None]
    cluster_delta = (
        gain_rows[:, None] * (jnp.exp(cluster_logit - top[:, None]) / total[:, None] - cluster_hot)
    ).astype(bf16)
    all_delta = lax.all_gather(head_delta, "dp", axis=0, tiled=True)
    all_cluster_delta = lax.all_gather(cluster_delta, "dp", axis=0, tiled=True)
    token_partial = lax.dot_general(
        head_delta, head_weight, (((1,), (1,)), ((), ())), preferred_element_type=f32
    ) + cluster_delta.astype(f32) * cluster_weight.astype(f32).T

    word_top = jnp.max(word_logits, axis=1, keepdims=True)
    word_exp = jnp.exp(word_logits - word_top)
    word_prob = word_exp / jnp.sum(word_exp, axis=1, keepdims=True)
    word_columns = jnp.arange(word_logits.shape[1], dtype=jnp.int32)
    word_hot = (word_columns[None, :] == own_words[:, None]).astype(f32)
    own_word_delta = (own_gains[:, None] * (word_prob - word_hot)).astype(bf16)
    word_delta = lax.all_gather(own_word_delta, "dp", axis=0, tiled=True)
    reduced_grad = lax.dot_general(
        word_delta, out, (((1,), (1,)), ((), ())), preferred_element_type=f32
    ).astype(bf16)
    tail_partial = lax.dot_general(
        reduced_grad, proj, (((1,), (1,)), ((), ())), preferred_element_type=f32
    )
    tail_sum = lax.psum_scatter(
        tail_partial.astype(bf16), "dp", scatter_dimension=0, tiled=True
    )
    out_grad = lax.dot_general(
        reduced, word_delta, (((0,), (0,)), ((), ())), preferred_element_type=f32
    ).astype(bf16)
    proj_grad = lax.dot_general(
        tail_rows, reduced_grad, (((0,), (0,)), ((), ())), preferred_element_type=f32
    ).astype(bf16)

    hidden_columns = lax.dynamic_slice_in_dim(all_hidden, dp_index * share, share, 1)
    head_grad = lax.dot_general(
        hidden_columns, all_delta, (((0,), (0,)), ((), ())), preferred_element_type=f32
    ).astype(bf16)
    cluster_grad = lax.dot_general(
        hidden_columns, all_cluster_delta, (((0,), (0,)), ((), ())), preferred_element_type=f32
    ).astype(bf16)

    spread_back = lax.dot_general(
        own_select.astype(bf16), tail_sum, (((0,), (0,)), ((), ())), preferred_element_type=f32
    )
    hidden_grad = lax.psum_scatter(
        token_partial + spread_back, "vocab", scatter_dimension=0, tiled=True
    ).astype(bf16)
    return (hidden_grad, head_grad, cluster_grad, proj_grad[None], out_grad[None])


def solution(mesh):
    placed = (
        P(("dp", "vocab"), None),
        P(("dp", "vocab")),
        P(("dp", "vocab")),
        P(None, "vocab"),
        P(None, "vocab"),
        P("vocab", None, "dp"),
        P("vocab", "dp", None),
    )
    return jax.shard_map(
        shards,
        mesh=mesh,
        in_specs=placed,
        out_specs=(
            P(("dp", "vocab"), None),
            P("dp", "vocab"),
            P("dp", "vocab"),
            P("vocab", None, "dp"),
            P("vocab", "dp", None),
        ),
        check_vma=False,
    )
```

time: 332 us -> 199 us (0.60)
  waiting for transfers between devices: 175 us -> 47.9 us
  local copies, waits for them, and re-layouts: 12.7 us -> 3.28 us
  blocking collectives: 80.7 us -> 86.9 us
    reduce_scatter x3, waiting for transfers between devices: 144 us -> 30.1 us  [the longest x1 15.8 us: shards(): lax.psum_scatter(tail_partial.astype(bf16), 'dp', scatter_dimension=0, ti...]
    all_gather x2 -> x4, blocking collectives: 27.5 us -> 78 us  [the longest x1 43.3 us: shards(): lax.all_gather(jnp.stack([targets.astype(f32), loss_weight.astype(f32)]),...]
    unnamed x5 -> x1, blocking collectives: 53.2 us -> 8.9 us
    unnamed x6 -> x4, waiting for transfers between devices: 22.3 us -> 0.73 us
    all_gather x0 -> x1, waiting for transfers between devices: none -> 17.1 us  [shards(): all_hidden = lax.all_gather(hidden, ('dp', 'vocab'), axis=0, tiled=True)]
    psum x1 -> x0, waiting for transfers between devices: 8.47 us -> none  [shards(): word_logits = lax.psum(partial_logits, 'dp')]
    unnamed x46 -> x21, local copies, waits for them, and re-layouts: 10.8 us -> 2.41 us
  transfers between devices with their start and end apart: 5 -> 4, of which waited for: 5 -> 4; matrix products, arithmetic and copies ran while one was open for 12% -> 15% of each run, Pallas kernels for 0% -> 0%
where the time goes in v1:
time: 199 us
  blocking collectives  86.9 us (44%)
  waiting for transfers between devices  47.9 us (24%)
  matrix products  37.8 us (19%)
  between operations  14.6 us (7%)
  other arithmetic  7.82 us (4%)
  local copies, waits for them, and re-layouts  3.28 us (2%)
    all_gather x1, blocking collectives, shards(): lax.all_gather(jnp.stack([targets.astype(f32), loss_weight.astype(f32)]),...  43.3 us
    all_gather x1, waiting for transfers between devices, shards(): all_hidden = lax.all_gather(hidden, ('dp', 'vocab'), axis=0, tiled=True)  17.1 us
    reduce_scatter x1, waiting for transfers between devices, shards(): lax.psum_scatter(tail_partial.astype(bf16), 'dp', scatter_dimension=0, ti...  15.8 us
    reduce_scatter x1, waiting for transfers between devices, shards(): lax.psum_scatter(partial_logits, 'dp', scatter_dimension=0, tiled=True)  14.1 us
    all_gather x1, blocking collectives, shards(): word_delta = lax.all_gather(own_word_delta, 'dp', axis=0, tiled=True)  12.9 us
    all_gather x1, blocking collectives, shards(): all_delta = lax.all_gather(head_delta, 'dp', axis=0, tiled=True)  11.1 us
    all_gather x1, blocking collectives, shards(): stats = lax.all_gather(jnp.stack([top, total]), 'vocab')  10.6 us
    unnamed x1, blocking collectives  8.9 us
  transfers between devices with their start and end apart: 4, of which 4 were waited for; matrix products, arithmetic and copies ran while one was open for 15% of the time, Pallas kernels for 0%

profile of v1, /device:TPU:0, one launch (start us, length us, event | category | flops | bytes accessed | tf_op | source)
XLA Modules:
  0.0 198.5 jit_solution(1393579287363786409)
XLA Ops:
  7.2 0.7 all-gather.6.cloned.1.call-update
  8.0 0.7 convert_bitcast_fusion
  8.6 0.7 bitcast_convert_fusion
  9.3 43.3 %all-gather.2 = f32[32,8,2]{1,2,0:T(2,128)S(1)} all-gather(f32[1,8,2]{1,2,0:T(2,128)S(1)} %maximum_bitcast_fusion), channel_id=1, replica_groups=mesh['dp'=4,'vocab'=8] {'dp','vocab'}, dimensions={0}, use_global_device_ids=true | all-gather | bytes 2112 | tf_op jit(solution)/shard_map/all_gather | solution.py:22
  53.2 17.1 %all-gather.6.cloned.1.call-done = bf16[256,4096]{1,0:T(8,128)(2,1)} async-done(((bf16[8,4096]{1,0:T(8,128)(2,1)}), bf16[256,4096]{1,0:T(8,128)(2,1)}) %all-gather.6.cloned.1.call-update) | async-done | bytes 2097168 | tf_op jit(solution)/shard_map/all_gather | solution.py:28
  70.3 2.1 %convolution_convert_fusion.3 = bf16[4,16,4096]{2,1,0:T(8,128)(2,1)S(1)} fusion(bf16[4,64,4096]{2,1,0:T(8,128)(2,1)} %bitcast.76, s32[4,64]{1,0:T(4,128)S(1)} %convert_reduce_fusion, pred[4,64]{1,0:T(4,128)(4,1)S(1)} %fusion.26), kind=kOutput, calls=%fused_computation.7 | convolution fusion | flops 33824768 | bytes 2622720 | tf_op jit(solution)/shard_map/ahw,awo->aho/dot_general | solution.py:47
  72.4 0.8 copy-done.2
  73.2 0.5 fusion.12
  73.7 2.1 %fusion.4 = f32[64,7680]{1,0:T(8,128)} fusion(bf16[64,256]{1,0:T(8,128)(2,1)S(1)} %fusion.12, bf16[1,256,7680]{2,1,0:T(8,128)(2,1)S(1)} %copy-done.1), kind=kOutput, calls=%fused_computation.10 | convolution fusion | flops 251658240 | bytes 5931008 | tf_op jit(solution)/shard_map/dot_general | solution.py:55
  76.2 6.2 %fusion.42 = (f32[64]{0:T(128)S(1)}, f32[64,1280]{1,0:T(8,128)S(1)}) fusion(bf16[4096,1280]{1,0:T(8,128)(2,1)} %param.10, bf16[256,4096]{1,0:T(8,128)(2,1)} %all-gather.6.cloned.1.call-done, s32[]{:T(128)S(6)} %select_n.45), kind=kOutput, calls=%fused_computation.74 | convolution fusion | flops 671170496 | bytes 11337988 | tf_op jit(solution)/shard_map/dot_general | solution.py:58
  82.4 1.3 fusion.43
  83.9 10.6 %all-gather.3 = f32[8,2,64]{2,1,0:T(2,128)S(1)} all-gather(f32[1,2,64]{2,1,0:T(2,128)S(1)} %maximum_bitcast_fusion.1), channel_id=2, replica_groups=mesh['dp'=4,'vocab'=8] {'vocab'}, dimensions={0}, use_global_device_ids=true | all-gather | bytes 4608 | tf_op jit(solution)/shard_map/all_gather | solution.py:66
  94.8 14.1 %reduce-scatter.4.cloned.1.call-done = f32[16,7680]{1,0:T(8,128)} async-done(((f32[64,7680]{1,0:T(8,128)}), f32[16,7680]{1,0:T(8,128)}) %reduce-scatter.4.cloned.1.call-update) | async-done | bytes 491536 | tf_op jit(solution)/shard_map/reduce_scatter | solution.py:56
  108.9 1.2 reduce_max.29
  110.1 1.3 fusion.21
  111.4 1.2 multiply_convert_fusion
  112.6 12.9 %all_gather.25 = bf16[64,7680]{1,0:T(8,128)(2,1)S(1)} all-gather(bf16[16,7680]{1,0:T(8,128)(2,1)S(1)} %multiply_convert_fusion), channel_id=1, replica_groups=mesh['dp'=4,'vocab'=8] {'dp'}, dimensions={0}, use_global_device_ids=true | all-gather | bytes 1228800 | tf_op jit(solution)/shard_map/all_gather | solution.py:89
  125.6 3.4 %fusion.9 = bf16[64,256]{1,0:T(8,128)(2,1)S(1)} fusion(bf16[64,7680]{1,0:T(8,128)(2,1)S(1)} %all_gather.25, bf16[1,256,7680]{2,1,0:T(8,128)(2,1)} %param.13), kind=kOutput, calls=%fused_computation.16 | convolution fusion | flops 251674624 | bytes 4947968 | tf_op jit(solution)/shard_map/dot_general | solution.py:90
  129.0 1.6 convolution_convert_fusion.2
  130.8 0.7 copy-done.4
  131.4 8.2 %convolution_add_fusion.1 = f32[64,4096]{1,0:T(8,128)} fusion(bf16[64,1280]{1,0:T(8,128)(2,1)S(1)} %multiply_convert_fusion.1, bf16[4096,1280]{1,0:T(8,128)(2,1)} %param.10, f32[4096]{0:T(1024)S(1)} %mul.60, f32[64]{0:T(128)S(1)} %get-tuple-element.7), kind=kOutput, calls=%fused_computation.5 | convolution fusion | flops 671612928 | bytes 11714816 | tf_op jit(solution)/shard_map/dot_general | solution.py:79
  139.6 15.8 %reduce-scatter.6.cloned.1.call-done = bf16[16,4096]{1,0:T(8,128)(2,1)} async-done(((bf16[64,4096]{1,0:T(8,128)(2,1)}), bf16[16,4096]{1,0:T(8,128)(2,1)}) %reduce-scatter.6.cloned.1.call-update) | async-done | bytes 131088 | tf_op jit(solution)/shard_map/reduce_scatter | solution.py:96
  155.5 2.6 %convolution_add_fusion = f32[64,4096]{1,0:T(8,128)} fusion(f32[64,4096]{1,0:T(8,128)} %convolution_add_fusion.1, bf16[16,4096]{1,0:T(8,128)(2,1)} %reduce-scatter.6.cloned.1.call-done, pred[4,16,64]{2,1,0:T(8,128)(4,1)S(1)} %fusion.22, s32[]{:T(128)S(6)} %select_n.49), kind=kOutput, calls=%fused_computation.4 | convolution fusion | flops 8650752 | bytes 2230276 | tf_op jit(solution)/shard_map/dot_general | solution.py:114
  158.1 0.6 dynamic-slice.2
  159.6 8.9 %all-reduce = bf16[256]{0:T(256)(128)(2,1)S(1)} all-reduce(bf16[256]{0:T(256)(128)(2,1)S(1)} %dynamic-update-slice), channel_id=3, replica_groups=mesh['dp'=4,'vocab'=8] {'dp'}, use_global_device_ids=true, to_apply=%add | all-reduce | flops 256 | bytes 1024
  168.5 1.2 fusion.15
  169.8 0.6 convert_element_type.93
  170.4 11.1 %all_gather.26 = bf16[256,1280]{1,0:T(8,128)(2,1)S(1)} all-gather(bf16[64,1280]{1,0:T(8,128)(2,1)S(1)} %copy-done.5), channel_id=1, replica_groups=mesh['dp'=4,'vocab'=8] {'dp'}, dimensions={0}, use_global_device_ids=true | all-gather | bytes 819200 | tf_op jit(solution)/shard_map/all_gather | solution.py:77
  181.5 3.5 %convolution_convert_fusion.4 = bf16[1024,1280]{1,0:T(8,128)(2,1)} fusion(bf16[256,1280]{1,0:T(8,128)(2,1)S(1)} %all_gather.26, bf16[256,4096]{1,0:T(8,128)(2,1)} %all-gather.6.cloned.1.call-done, s32[]{:T(128)S(6)} %select_n.53), kind=kOutput, calls=%fused_computation.12 | convolution fusion | flops 672399360 | bytes 3801092 | tf_op jit(solution)/shard_map/dot_general | solution.py:107
  185.0 2.1 %fusion.1 = bf16[1,4096,256]{2,1,0:T(8,128)(2,1)} fusion(bf16[64,4096]{1,0:T(8,128)(2,1)S(1)} %bitcast.78, bf16[64,256]{1,0:T(8,128)(2,1)S(1)} %fusion.9), kind=kOutput, calls=%fused_computation.3 | convolution fusion | flops 135266304 | bytes 2654208 | tf_op jit(solution)/shard_map/dot_general | solution.py:102
  187.0 3.1 %fusion = bf16[1,256,7680]{2,1,0:T(8,128)(2,1)} fusion(bf16[64,256]{1,0:T(8,128)(2,1)S(1)} %fusion.12, bf16[64,7680]{1,0:T(8,128)(2,1)S(1)} %all_gather.25), kind=kOutput, calls=%fused_computation.1 | convolution fusion | flops 253624320 | bytes 4947968 | tf_op jit(solution)/shard_map/dot_general | solution.py:99
  190.4 1.5 convert_element_type.89
  (52 shorter events, 2.3 us)
Async XLA Ops:
  7.2 66.1 %copy-start = (bf16[1,4096,256]{2,1,0:T(8,128)(2,1)S(1)}, bf16[1,4096,256]{2,1,0:T(8,128)(2,1)}, u32[]{:S(2)}) copy-start(bf16[1,4096,256]{2,1,0:T(8,128)(2,1)} %param.12) | copy-start | bytes 6291460
  7.2 63.1 %all-gather.6.cloned.1.call-start = ((), (), s32[]{:S(2)}) async-start(), calls=%async_computation.3 | async-start | bytes 2162688 | tf_op jit(solution)/shard_map/all_gather | solution.py:28
  7.9 101.0 %reduce-scatter.4.cloned.1.call-start = ((), (), s32[]{:S(2)}) async-start(), calls=%async_computation.4 | async-start | bytes 2457600 | tf_op jit(solution)/shard_map/reduce_scatter | solution.py:56
  70.3 3.4 %copy-start.1 = (bf16[1,256,7680]{2,1,0:T(8,128)(2,1)S(1)}, bf16[1,256,7680]{2,1,0:T(8,128)(2,1)}, u32[]{:S(2)}) copy-start(bf16[1,256,7680]{2,1,0:T(8,128)(2,1)} %param.13) | copy-start | bytes 11796484
  72.4 0.8 copy-start.2
  73.7 2.2 %copy-start.6 = (bf16[4096,1]{0,1:T(2,128)(2,1)S(1)}, bf16[4096,1]{0,1:T(2,128)(2,1)}, u32[]{:S(2)}) copy-start(bf16[4096,1]{0,1:T(2,128)(2,1)} %param.11) | copy-start | bytes 24580
  75.8 79.6 %reduce-scatter.6.cloned.1.call-start = ((), (), s32[]{:S(2)}) async-start(), calls=%async_computation.5 | async-start | bytes 655360 | tf_op jit(solution)/shard_map/reduce_scatter | solution.py:96
  130.5 59.9 %reduce-scatter.8.cloned.1.call-start = ((), (), s32[]{:S(2)}) async-start(), calls=%async_computation.6 | async-start | bytes 1179648 | tf_op jit(solution)/shard_map/reduce_scatter | solution.py:117
  130.8 0.7 copy-start.4
  139.6 18.5 %copy-start.7 = (u32[32]{0:T(128)S(1)}, u32[32]{0:T(128)}, u32[]{:S(2)}) copy-start(u32[32]{0:T(128)} %constant.72) | copy-start | bytes 388
  139.6 30.7 %copy-start.5 = (bf16[64,1280]{1,0:T(8,128)(2,1)S(1)}, bf16[64,1280]{1,0:T(8,128)(2,1)}, u32[]{:S(2)}) copy-start(bf16[64,1280]{1,0:T(8,128)(2,1)} %copy-done.4) | copy-start | bytes 491524
  181.5 3.5 %copy-start.3 = (bf16[4,16,4096]{2,1,0:T(8,128)(2,1)S(1)}, bf16[4,16,4096]{2,1,0:T(8,128)(2,1)}, u32[]{:S(2)}) copy-start(bf16[4,16,4096]{2,1,0:T(8,128)(2,1)} %copy-done.2) | copy-start | bytes 1572868
Sparse Core Ops, SparseCore 0:
  11.0 59.2 all-gather.5
  75.9 32.9 reduce-scatter.3
  130.7 24.7 reduce-scatter.5
  158.2 32.1 reduce-scatter.7

commit v2 on v1

v2 whole, which is shorter than its diff:
```python
import functools

import jax
import jax.numpy as jnp
from jax import lax
from jax.experimental import pallas as pl
from jax.experimental.pallas import tpu as pltpu
from jax.sharding import PartitionSpec as P

HEAD = 10240
CV = 7680
CLUSTER_TOKEN_CAP = 16
MESH = pl.DeviceIdType.MESH
VMEM_LIMIT = 56 * 2**20


def remote(src, dst, send, recv, axis, peer):
    return pltpu.make_async_remote_copy(
        src_ref=src, dst_ref=dst, send_sem=send, recv_sem=recv,
        device_id={axis: peer}, device_id_type=MESH,
    )


def greet(axis, peers):
    barrier = pltpu.get_barrier_semaphore()
    for peer in peers:
        pl.semaphore_signal(barrier, inc=1, device_id={axis: peer}, device_id_type=MESH)
    pl.semaphore_wait(barrier, len(peers))


def call(body, operands, results, scratch, collective_id):
    vmem = pl.BlockSpec(memory_space=pltpu.VMEM)
    return pl.pallas_call(
        body,
        out_shape=results,
        in_specs=[vmem] * len(operands),
        out_specs=[vmem] * len(results),
        scratch_shapes=scratch,
        compiler_params=pltpu.CompilerParams(
            collective_id=collective_id, has_side_effects=True, vmem_limit_bytes=VMEM_LIMIT
        ),
    )(*operands)


def exchange_body(axis, n, split, count, *refs):
    ins, outs = refs[:count], refs[count : 2 * count]
    send, recv, local = refs[2 * count :]
    me = lax.axis_index(axis)
    peers = [lax.rem(me + k, n) for k in range(1, n)]
    greet(axis, peers)
    copies = []
    for i in range(count):
        for k, peer in enumerate(peers):
            src = ins[i].at[peer] if split[i] else ins[i]
            copy = remote(src, outs[i].at[me], send.at[i, k], recv.at[i, k], axis, peer)
            copy.start()
            copies.append(copy)
    for i in range(count):
        src = ins[i].at[me] if split[i] else ins[i]
        copy = pltpu.make_async_copy(src, outs[i].at[me], local.at[i])
        copy.start()
        copies.append(copy)
    for copy in copies:
        copy.wait()


def exchange(axis, gathers, splits, collective_id):
    n = lax.axis_size(axis)
    operands = [*gathers, *splits]
    count = len(operands)
    results = [jax.ShapeDtypeStruct((n, *a.shape), a.dtype) for a in gathers]
    results += [jax.ShapeDtypeStruct(a.shape, a.dtype) for a in splits]
    split = [False] * len(gathers) + [True] * len(splits)
    dma = pltpu.SemaphoreType.DMA
    return call(
        functools.partial(exchange_body, axis, n, split, count),
        operands, results,
        [dma((count, n - 1)), dma((count, n - 1)), dma((count,))],
        collective_id,
    )


def pair_gather_body(axis, n, count, *refs):
    ins, outs = refs[:count], refs[count : 2 * count]
    send, recv, pass_send, pass_recv, local = refs[2 * count :]
    half = n // 2
    me = lax.axis_index(axis)
    place, core = me // 2, lax.rem(me, 2)
    partner = 2 * place + 1 - core
    peers = [2 * lax.rem(place + k, half) + core for k in range(1, half)]
    greet(axis, peers + [partner])
    copies, passed = [], []
    for i in range(count):
        for k, peer in enumerate(peers):
            copy = remote(ins[i], outs[i].at[me], send.at[i, k], recv.at[i, k], axis, peer)
            copy.start()
            copies.append(copy)
        copy = remote(ins[i], outs[i].at[me], pass_send.at[i, 0], pass_recv.at[i, 0], axis, partner)
        copy.start()
        passed.append(copy)
        copy = pltpu.make_async_copy(ins[i], outs[i].at[me], local.at[i])
        copy.start()
        passed.append(copy)
    for k in range(1, half):
        source = 2 * lax.rem(place + half - k, half) + core
        for i in range(count):
            copies[i * (half - 1) + k - 1].wait_recv()
            block = outs[i].at[source]
            copy = remote(block, block, pass_send.at[i, k], pass_recv.at[i, k], axis, partner)
            copy.start()
            passed.append(copy)
    for copy in copies:
        copy.wait_send()
    for copy in passed:
        copy.wait()


def pair_gather(axis, operands, collective_id):
    n = lax.axis_size(axis)
    count = len(operands)
    dma = pltpu.SemaphoreType.DMA
    half = n // 2
    return call(
        functools.partial(pair_gather_body, axis, n, count),
        operands,
        [jax.ShapeDtypeStruct((n, *a.shape), a.dtype) for a in operands],
        [dma((count, half - 1)), dma((count, half - 1)), dma((count, half)), dma((count, half)), dma((count,))],
        collective_id,
    )


def pair_scatter_body(axis, n, x, out, theirs, mine, landed, send, recv, pair_send, pair_recv):
    half = n // 2
    me = lax.axis_index(axis)
    place, core = me // 2, lax.rem(me, 2)
    partner = 2 * place + 1 - core
    order = [lax.rem(place + k, half) for k in range(1, half)]
    greet(axis, [2 * p + core for p in order] + [partner])
    order = order + [place]
    pairs, copies = [], []
    for k, p in enumerate(order):
        copy = remote(x.at[2 * p + 1 - core], theirs.at[k], pair_send.at[k], pair_recv.at[k], axis, partner)
        copy.start()
        pairs.append(copy)
    for k, p in enumerate(order):
        pairs[k].wait_recv()
        mine[k] = x[2 * p + core] + theirs[k]
        if k < half - 1:
            copy = remote(mine.at[k], landed.at[k], send.at[k], recv.at[k], axis, 2 * p + core)
            copy.start()
            copies.append(copy)
    total = mine[half - 1]
    for k, copy in enumerate(copies):
        copy.wait_recv()
        total = total + landed[k]
    out[...] = total
    for copy in pairs + copies:
        copy.wait_send()


def pair_scatter(axis, x, collective_id):
    n = lax.axis_size(axis)
    half = n // 2
    block = x.shape[1:]
    dma = pltpu.SemaphoreType.DMA
    return call(
        functools.partial(pair_scatter_body, axis, n),
        [x], [jax.ShapeDtypeStruct(block, x.dtype)],
        [
            pltpu.VMEM((half, *block), x.dtype),
            pltpu.VMEM((half, *block), x.dtype),
            pltpu.VMEM((half - 1, *block), x.dtype),
            dma((half - 1,)), dma((half - 1,)), dma((half,)), dma((half,)),
        ],
        collective_id,
    )[0]


def lanes(rows):
    x = jnp.stack([r.astype(jnp.float32) for r in rows])
    return jnp.pad(x, ((0, -x.shape[0] % 8), (0, -x.shape[1] % 128)))


def shards(hidden, targets, loss_weight, head_weight, cluster_weight, tail_proj, tail_out):
    vocab_index = lax.axis_index("vocab")
    n_dp = lax.axis_size("dp")
    n_vocab = lax.axis_size("vocab")
    local, model = hidden.shape
    span = local * n_vocab
    share = model // n_dp
    cap = CLUSTER_TOKEN_CAP
    f32, bf16 = jnp.float32, jnp.bfloat16

    held, facts = pair_gather(
        "vocab", [hidden.reshape(2 * local, model // 2), lanes([targets, loss_weight])], 1
    )
    rows_hidden = held.reshape(span, model)
    row_targets = facts[:, 0, :local].reshape(span).astype(jnp.int32)
    gain_rows = facts[:, 1, :local].reshape(span)

    offset = row_targets - HEAD
    member = (offset >= 0) & (offset // CV == vocab_index)
    place = jnp.arange(span, dtype=jnp.int32)
    rank = jnp.sum((member[None, :] & (place[None, :] < place[:, None])).astype(jnp.int32), axis=1)
    slots = jnp.arange(cap, dtype=jnp.int32)
    own_select = member[None, :] & (rank[None, :] == slots[:, None])
    own_words = jnp.sum(jnp.where(own_select, offset[None, :] % CV, 0), axis=1).astype(jnp.int32)
    own_gains = jnp.sum(jnp.where(own_select, gain_rows[None, :], 0.0), axis=1)
    own_rows = jnp.dot(own_select.astype(bf16), rows_hidden, preferred_element_type=f32).astype(bf16)
    pieces = rows_hidden.reshape(span, n_dp, share).transpose(1, 0, 2)
    tail_rows, hidden_columns = exchange("dp", [own_rows], [pieces], 2)
    tail_rows = tail_rows.reshape(n_dp * cap, model)
    hidden_columns = hidden_columns.reshape(n_dp * span, share)

    proj = tail_proj[0]
    out = tail_out[0]
    reduced = jnp.dot(tail_rows, proj, preferred_element_type=f32).astype(bf16)
    partial_logits = jnp.dot(reduced, out, preferred_element_type=f32)
    word_logits = lax.psum_scatter(partial_logits, "dp", scatter_dimension=0, tiled=True)

    local_logits = jnp.dot(rows_hidden, head_weight, preferred_element_type=f32)
    cluster_logit = jnp.dot(rows_hidden, cluster_weight, preferred_element_type=f32)
    width = head_weight.shape[1]
    columns = vocab_index * width + jnp.arange(width, dtype=jnp.int32)
    row_offset = row_targets - HEAD
    target_column = jnp.where(row_offset >= 0, HEAD + row_offset // CV, row_targets)
    top = jnp.maximum(jnp.max(local_logits, axis=1), cluster_logit[:, 0])
    total = jnp.sum(jnp.exp(local_logits - top[:, None]), axis=1) + jnp.exp(cluster_logit[:, 0] - top)
    (stats,) = exchange("vocab", [lanes([top, total])], [], 3)
    tops, totals = stats[:, 0, :span], stats[:, 1, :span]
    top = jnp.max(tops, axis=0)
    total = jnp.sum(totals * jnp.exp(tops - top[None, :]), axis=0)
    head_hot = (columns[None, :] == target_column[:, None]).astype(f32)
    head_delta = (
        gain_rows[:, None] * (jnp.exp(local_logits - top[:, None]) / total[:, None] - head_hot)
    ).astype(bf16)
    cluster_hot = (target_column == HEAD + vocab_index).astype(f32)[:, None]
    cluster_delta = (
        gain_rows[:, None] * (jnp.exp(cluster_logit - top[:, None]) / total[:, None] - cluster_hot)
    ).astype(bf16)
    token_partial = lax.dot_general(
        head_delta, head_weight, (((1,), (1,)), ((), ())), preferred_element_type=f32
    ) + cluster_delta.astype(f32) * cluster_weight.astype(f32).T

    word_top = jnp.max(word_logits, axis=1, keepdims=True)
    word_exp = jnp.exp(word_logits - word_top)
    word_prob = word_exp / jnp.sum(word_exp, axis=1, keepdims=True)
    word_columns = jnp.arange(word_logits.shape[1], dtype=jnp.int32)
    word_hot = (word_columns[None, :] == own_words[:, None]).astype(f32)
    own_word_delta = (own_gains[:, None] * (word_prob - word_hot)).astype(bf16)
    deltas = jnp.concatenate([head_delta, cluster_delta], axis=1)
    deltas = jnp.pad(deltas, ((0, 0), (0, -deltas.shape[1] % 128)))
    word_delta, deltas = exchange("dp", [own_word_delta, deltas], [], 4)
    word_delta = word_delta.reshape(n_dp * cap, -1)
    deltas = deltas.reshape(n_dp * span, -1)
    all_delta, all_cluster_delta = deltas[:, :width], deltas[:, width : width + 1]
    reduced_grad = lax.dot_general(
        word_delta, out, (((1,), (1,)), ((), ())), preferred_element_type=f32
    ).astype(bf16)
    tail_partial = lax.dot_general(
        reduced_grad, proj, (((1,), (1,)), ((), ())), preferred_element_type=f32
    )
    (tail_parts,) = exchange("dp", [], [tail_partial.astype(bf16).reshape(n_dp, cap, model)], 5)
    tail_sum = jnp.sum(tail_parts.astype(f32), axis=0).astype(bf16)
    out_grad = lax.dot_general(
        reduced, word_delta, (((0,), (0,)), ((), ())), preferred_element_type=f32
    ).astype(bf16)
    proj_grad = lax.dot_general(
        tail_rows, reduced_grad, (((0,), (0,)), ((), ())), preferred_element_type=f32
    ).astype(bf16)

    head_grad = lax.dot_general(
        hidden_columns, all_delta, (((0,), (0,)), ((), ())), preferred_element_type=f32
    ).astype(bf16)
    cluster_grad = lax.dot_general(
        hidden_columns, all_cluster_delta, (((0,), (0,)), ((), ())), preferred_element_type=f32
    ).astype(bf16)

    spread_back = lax.dot_general(
        own_select.astype(bf16), tail_sum, (((0,), (0,)), ((), ())), preferred_element_type=f32
    )
    partial = (token_partial + spread_back).reshape(n_vocab, local, model)
    hidden_grad = pair_scatter("vocab", partial, 6).astype(bf16)
    return (hidden_grad, head_grad, cluster_grad, proj_grad[None], out_grad[None])


def solution(mesh):
    placed = (
        P(("dp", "vocab"), None),
        P(("dp", "vocab")),
        P(("dp", "vocab")),
        P(None, "vocab"),
        P(None, "vocab"),
        P("vocab", None, "dp"),
        P("vocab", "dp", None),
    )
    return jax.shard_map(
        shards,
        mesh=mesh,
        in_specs=placed,
        out_specs=(
            P(("dp", "vocab"), None),
            P("dp", "vocab"),
            P("dp", "vocab"),
            P("vocab", None, "dp"),
            P("vocab", "dp", None),
        ),
        check_vma=False,
    )
```

time: 199 us -> 167 us (0.84)
  Pallas kernels: 0 us -> 88.5 us
  blocking collectives: 86.9 us -> 0 us
  waiting for transfers between devices: 47.9 us -> 9.84 us
  matrix products: 37.8 us -> 32.4 us
  other arithmetic: 7.82 us -> 12.3 us
  local copies, waits for them, and re-layouts: 3.28 us -> 7.57 us
    pallas_call x0 -> x6, Pallas kernels: none -> 88.5 us  [call(): pl.pallas_call(body, out_shape=results, in_specs=[vmem] * len(operands),...]
    all_gather x4 -> x0, blocking collectives: 78 us -> none  [the longest x1 43.3 us: shards(): lax.all_gather(jnp.stack([targets.astype(f32), loss_weight.astype(f32)]),...]
    all_gather x1 -> x0, waiting for transfers between devices: 17.1 us -> none  [shards(): all_hidden = lax.all_gather(hidden, ('dp', 'vocab'), axis=0, tiled=True)]
    reduce_scatter x2 -> x0, waiting for transfers between devices: 16.1 us -> none  [the longest x1 15.8 us: shards(): lax.psum_scatter(tail_partial.astype(bf16), 'dp', scatter_dimension=0, ti...]
    unnamed x1 -> x0, blocking collectives: 8.9 us -> none
    reduce_scatter x1, waiting for transfers between devices: 14.1 us -> 9.82 us  [shards(): lax.psum_scatter(partial_logits, 'dp', scatter_dimension=0, tiled=True)]
    reshape x0 -> x2, local copies, waits for them, and re-layouts: none -> 2.71 us  [the longest x1 1.49 us: shards(): hidden.reshape(2 * local, model // 2)]
    unnamed x21 -> x12, local copies, waits for them, and re-layouts: 2.41 us -> 0.03 us
  transfers between devices with their start and end apart: 4 -> 1, of which waited for: 4 -> 1; matrix products, arithmetic and copies ran while one was open for 15% -> 11% of each run, Pallas kernels for 0% -> 4%
where the time goes in v2:
time: 167 us; the launch traced here: 165 us
  Pallas kernels  88.5 us (53%)
  matrix products  32.4 us (19%)
  between operations  14.2 us (9%)
  other arithmetic  12.3 us (7%)
  waiting for transfers between devices  9.84 us (6%)
  local copies, waits for them, and re-layouts  7.57 us (5%)
    pallas_call x6, Pallas kernels, call(): pl.pallas_call(body, out_shape=results, in_specs=[vmem] * len(operands),...  88.5 us
    reduce_scatter x1, waiting for transfers between devices, shards(): lax.psum_scatter(partial_logits, 'dp', scatter_dimension=0, tiled=True)  9.82 us
    dot_general x1, matrix products, shards(): lax.dot_general(head_delta, head_weight, (((1,), (1,)), ((), ())), prefer...  7.35 us
    dot_general x1, matrix products, shards(): local_logits = jnp.dot(rows_hidden, head_weight, preferred_element_type=f32)  5.99 us
    dot_general x1, matrix products, shards(): lax.dot_general(hidden_columns, all_delta, (((0,), (0,)), ((), ())), pref...  3.65 us
  transfers between devices with their start and end apart: 1, of which 1 were waited for; matrix products, arithmetic and copies ran while one was open for 11% of the time, Pallas kernels for 4%

profile of v2, /device:TPU:0, one launch (start us, length us, event | category | flops | bytes accessed | tf_op | source)
XLA Modules:
  0.0 164.8 jit_solution(11703357413746148993)
XLA Ops:
  7.2 0.8 convert_bitcast_fusion.1
  8.7 1.5 reshape.117.refs_0_
  10.8 14.8 %shard_map.110 = (bf16[8,16,2048]{2,1,0:T(8,128)(2,1)}, f32[8,8,128]{2,1,0:T(8,128)}) custom-call(bf16[16,2048]{1,0:T(8,128)(2,1)} %reshape.117.refs_0_, f32[8,128]{1,0:T(8,128)} %select_maximum_fusion.1.refs_1_), custom_call_target="tpu_custom_call" | custom-call | tf_op jit(solution)/shard_map/pallas_call | solution.py:33
  25.5 1.2 reshape.118
  26.8 1.4 reshape_reshape.3
  28.1 0.8 convert_reduce_fusion.1
  29.1 1.0 copy.25
  30.1 0.8 convolution_convert_fusion.3.refs_0_
  30.9 17.5 %shard_map.112 = (bf16[4,16,4096]{2,1,0:T(8,128)(2,1)}, bf16[4,64,1024]{2,1,0:T(8,128)(2,1)}) custom-call(bf16[16,4096]{1,0:T(8,128)(2,1)} %convolution_convert_fusion.3.refs_0_, bf16[4,64,1024]{2,1,0:T(8,128)(2,1)} %bitcast.66), custom_call_target="tpu_custom_call" | custom-call | tf_op jit(solution)/shard_map/pallas_call | solution.py:33
  48.4 1.5 fusion.13
  50.0 2.1 %fusion.5 = f32[64,7680]{1,0:T(8,128)} fusion(bf16[64,256]{1,0:T(8,128)(2,1)S(1)} %fusion.13, bf16[1,256,7680]{2,1,0:T(8,128)(2,1)S(1)} %copy-done.1), kind=kOutput, calls=%fused_computation.11 | convolution fusion | flops 251658240 | bytes 5931008 | tf_op jit(solution)/shard_map/dot_general | solution.py:218
  52.2 0.8 slice_reduce_fusion
  53.0 6.0 %fusion.36 = (f32[64]{0:T(128)S(1)}, f32[64,1280]{1,0:T(8,128)S(1)}) fusion(bf16[64,4096]{1,0:T(8,128)(2,1)S(1)} %reshape.118, bf16[4096,1280]{1,0:T(8,128)(2,1)} %param.10), kind=kOutput, calls=%fused_computation.69 | convolution fusion | flops 671170496 | bytes 11337984 | tf_op jit(solution)/shard_map/dot_general | solution.py:221
  60.1 6.8 %shard_map.111 = f32[8,8,128]{2,1,0:T(8,128)} custom-call(f32[8,128]{1,0:T(8,128)} %select_maximum_fusion.refs_0_), custom_call_target="tpu_custom_call" | custom-call | tf_op jit(solution)/shard_map/pallas_call | solution.py:33
  67.0 0.8 fusion.35
  69.1 7.4 %convolution_add_fusion.1 = f32[64,4096]{1,0:T(8,128)S(1)} fusion(bf16[64,1280]{1,0:T(8,128)(2,1)S(1)} %multiply_convert_fusion.1, bf16[4096,1280]{1,0:T(8,128)(2,1)} %param.10, f32[4096]{0:T(1024)S(1)} %mul.51, f32[64]{0:T(128)S(1)} %get-tuple-element.19), kind=kOutput, calls=%fused_computation.6 | convolution fusion | flops 671612928 | bytes 11714816 | tf_op jit(solution)/shard_map/dot_general | solution.py:241
  76.5 9.8 %reduce-scatter.2.cloned.1.call-done = f32[16,7680]{1,0:T(8,128)} async-done(((f32[64,7680]{1,0:T(8,128)}), f32[16,7680]{1,0:T(8,128)}) %reduce-scatter.2.cloned.1.call-update) | async-done | bytes 491536 | tf_op jit(solution)/shard_map/reduce_scatter | solution.py:219
  86.3 1.2 reduce_max.29
  87.5 1.4 fusion.17
  88.9 1.9 %multiply_convert_fusion.refs_0_ = bf16[16,7680]{1,0:T(8,128)(2,1)} fusion(f32[16,7680]{1,0:T(8,128)} %reduce-scatter.2.cloned.1.call-done, s32[16]{0:T(128)S(1)} %select_reduce_fusion, f32[16]{0:T(128)S(1)} %fusion.17, f32[16]{0:T(128)S(1)} %reduce_max.29, f32[16]{0:T(128)S(1)} %select_reduce_fusion.1), kind=kLoop, calls=%fused_computation.22 | loop fusion | flops 860160 | bytes 737536 | tf_op jit(solution)/shard_map/convert_element_type | solution.py:250
  90.9 24.0 %shard_map.113 = (bf16[4,16,7680]{2,1,0:T(8,128)(2,1)}, bf16[4,64,1408]{2,1,0:T(8,128)(2,1)}) custom-call(bf16[16,7680]{1,0:T(8,128)(2,1)} %multiply_convert_fusion.refs_0_, bf16[64,1408]{1,0:T(8,128)(2,1)} %fusion.20.refs_1_), custom_call_target="tpu_custom_call" | custom-call | tf_op jit(solution)/shard_map/pallas_call | solution.py:33
  114.9 1.3 fusion.21
  116.2 3.6 %convolution_convert_fusion.4 = bf16[1024,1280]{1,0:T(8,128)(2,1)} fusion(bf16[256,1024]{1,0:T(8,128)(2,1)} %bitcast.71, bf16[256,1408]{1,0:T(8,128)(2,1)} %bitcast.73), kind=kOutput, calls=%fused_computation.13 | convolution fusion | flops 672399360 | bytes 3801088 | tf_op jit(solution)/shard_map/dot_general | solution.py:272
  119.9 1.3 fusion.10
  121.2 1.5 convolution_convert_fusion.2
  122.7 2.1 %fusion.1 = bf16[1,4096,256]{2,1,0:T(8,128)(2,1)} fusion(bf16[64,4096]{1,0:T(8,128)(2,1)S(1)} %bitcast.69, bf16[64,256]{1,0:T(8,128)(2,1)S(1)} %fusion.10), kind=kOutput, calls=%fused_computation.3 | convolution fusion | flops 135266304 | bytes 2654208 | tf_op jit(solution)/shard_map/dot_general | solution.py:268
  124.8 3.1 %fusion = bf16[1,256,7680]{2,1,0:T(8,128)(2,1)} fusion(bf16[64,256]{1,0:T(8,128)(2,1)S(1)} %fusion.13, bf16[64,7680]{1,0:T(8,128)(2,1)S(1)} %bitcast.65), kind=kOutput, calls=%fused_computation.1 | convolution fusion | flops 253624320 | bytes 4947968 | tf_op jit(solution)/shard_map/dot_general | solution.py:265
  128.5 10.0 %shard_map.114 = bf16[4,16,4096]{2,1,0:T(8,128)(2,1)} custom-call(bf16[4,16,4096]{2,1,0:T(8,128)(2,1)} %bitcast.67), custom_call_target="tpu_custom_call" | custom-call | tf_op jit(solution)/shard_map/pallas_call | solution.py:33
  138.6 1.1 reduce_sum.72
  139.7 1.3 fusion.2.x
  141.0 15.4 %shard_map.115 = f32[8,4096]{1,0:T(8,128)} custom-call(f32[8,8,4096]{2,1,0:T(8,128)} %fusion.2.x), custom_call_target="tpu_custom_call" | custom-call | tf_op jit(solution)/shard_map/pallas_call | solution.py:33
  156.4 1.5 convert_element_type.106
  (38 shorter events, 4.7 us)
Async XLA Ops:
  7.2 41.3 %copy-start = (bf16[1,4096,256]{2,1,0:T(8,128)(2,1)S(1)}, bf16[1,4096,256]{2,1,0:T(8,128)(2,1)}, u32[]{:S(2)}) copy-start(bf16[1,4096,256]{2,1,0:T(8,128)(2,1)} %param.12) | copy-start | bytes 6291460
  7.2 79.1 %reduce-scatter.2.cloned.1.call-start = ((), (), s32[]{:S(2)}) async-start(), calls=%async_computation.1 | async-start | bytes 2457600 | tf_op jit(solution)/shard_map/reduce_scatter | solution.py:219
  29.0 20.9 %copy-start.1 = (bf16[1,256,7680]{2,1,0:T(8,128)(2,1)S(1)}, bf16[1,256,7680]{2,1,0:T(8,128)(2,1)}, u32[]{:S(2)}) copy-start(bf16[1,256,7680]{2,1,0:T(8,128)(2,1)} %param.13) | copy-start | bytes 11796484
  50.0 2.1 %copy-start.5 = (bf16[4096,1]{0,1:T(2,128)(2,1)S(1)}, bf16[4096,1]{0,1:T(2,128)(2,1)}, u32[]{:S(2)}) copy-start(bf16[4096,1]{0,1:T(2,128)(2,1)} %param.11) | copy-start | bytes 24580
  87.5 32.4 %copy-start.2 = (bf16[1,256,7680]{2,1,0:T(8,128)(2,1)S(1)}, bf16[1,256,7680]{2,1,0:T(8,128)(2,1)}, u32[]{:S(2)}) copy-start(bf16[1,256,7680]{2,1,0:T(8,128)(2,1)} %param.13) | copy-start | bytes 11796484
  114.9 5.0 %copy-start.3 = (bf16[4,16,7680]{2,1,0:T(8,128)(2,1)S(1)}, bf16[4,16,7680]{2,1,0:T(8,128)(2,1)}, u32[]{:S(2)}) copy-start(bf16[4,16,7680]{2,1,0:T(8,128)(2,1)} %get-tuple-element.14) | copy-start | bytes 2949124
  119.9 2.9 %copy-start.4 = (bf16[4,16,4096]{2,1,0:T(8,128)(2,1)S(1)}, bf16[4,16,4096]{2,1,0:T(8,128)(2,1)}, u32[]{:S(2)}) copy-start(bf16[4,16,4096]{2,1,0:T(8,128)(2,1)} %get-tuple-element.13) | copy-start | bytes 1572868
Sparse Core Ops, SparseCore 0:
  52.2 34.0 reduce-scatter.1

commit v3 on v2

--- a/solution.py
+++ b/solution.py
@@ -129,7 +129,7 @@
     )
 
 
-def pair_scatter_body(axis, n, x, out, theirs, mine, landed, send, recv, pair_send, pair_recv):
+def pair_scatter_body(axis, n, x, out, theirs, leaving, landed, send, recv, pair_send, pair_recv):
     half = n // 2
     me = lax.axis_index(axis)
     place, core = me // 2, lax.rem(me, 2)
@@ -144,15 +144,15 @@
         pairs.append(copy)
     for k, p in enumerate(order):
         pairs[k].wait_recv()
-        mine[k] = x[2 * p + core] + theirs[k]
+        total = x[2 * p + core] + theirs[k]
         if k < half - 1:
-            copy = remote(mine.at[k], landed.at[k], send.at[k], recv.at[k], axis, 2 * p + core)
+            leaving[k] = total.astype(leaving.dtype)
+            copy = remote(leaving.at[k], landed.at[k], send.at[k], recv.at[k], axis, 2 * p + core)
             copy.start()
             copies.append(copy)
-    total = mine[half - 1]
     for k, copy in enumerate(copies):
         copy.wait_recv()
-        total = total + landed[k]
+        total = total + landed[k].astype(total.dtype)
     out[...] = total
     for copy in pairs + copies:
         copy.wait_send()
@@ -168,12 +168,31 @@
         [x], [jax.ShapeDtypeStruct(block, x.dtype)],
         [
             pltpu.VMEM((half, *block), x.dtype),
-            pltpu.VMEM((half, *block), x.dtype),
-            pltpu.VMEM((half - 1, *block), x.dtype),
+            pltpu.VMEM((half - 1, *block), jnp.bfloat16),
+            pltpu.VMEM((half - 1, *block), jnp.bfloat16),
             dma((half - 1,)), dma((half - 1,)), dma((half,)), dma((half,)),
         ],
         collective_id,
     )[0]
+
+
+def turned(axis, k):
+    n = lax.axis_size(axis)
+    return [(i, (i + k) % n) for i in range(n)]
+
+
+def gather_turned(x, axis):
+    return [x] + [lax.ppermute(x, axis, turned(axis, k)) for k in range(1, lax.axis_size(axis))]
+
+
+def scatter_turned(x, axis):
+    n, me = lax.axis_size(axis), lax.axis_index(axis)
+    rows = x.shape[0] // n
+
+    def part(k):
+        return lax.dynamic_slice_in_dim(x, lax.rem(me + k, n) * rows, rows, 0)
+
+    return [part(0)] + [lax.ppermute(part(k), axis, turned(axis, k)) for k in range(1, n)]
 
 
 def lanes(rows):
@@ -207,16 +226,16 @@
     own_words = jnp.sum(jnp.where(own_select, offset[None, :] % CV, 0), axis=1).astype(jnp.int32)
     own_gains = jnp.sum(jnp.where(own_select, gain_rows[None, :], 0.0), axis=1)
     own_rows = jnp.dot(own_select.astype(bf16), rows_hidden, preferred_element_type=f32).astype(bf16)
-    pieces = rows_hidden.reshape(span, n_dp, share).transpose(1, 0, 2)
-    tail_rows, hidden_columns = exchange("dp", [own_rows], [pieces], 2)
+    (tail_rows,) = exchange("dp", [own_rows], [], 2)
     tail_rows = tail_rows.reshape(n_dp * cap, model)
-    hidden_columns = hidden_columns.reshape(n_dp * span, share)
 
     proj = tail_proj[0]
     out = tail_out[0]
     reduced = jnp.dot(tail_rows, proj, preferred_element_type=f32).astype(bf16)
     partial_logits = jnp.dot(reduced, out, preferred_element_type=f32)
-    word_logits = lax.psum_scatter(partial_logits, "dp", scatter_dimension=0, tiled=True)
+
+    rows_hidden, partial_logits = lax.optimization_barrier((rows_hidden, partial_logits))
+    logit_parts = scatter_turned(partial_logits, "dp")
 
     local_logits = jnp.dot(rows_hidden, head_weight, preferred_element_type=f32)
     cluster_logit = jnp.dot(rows_hidden, cluster_weight, preferred_element_type=f32)
@@ -242,17 +261,22 @@
         head_delta, head_weight, (((1,), (1,)), ((), ())), preferred_element_type=f32
     ) + cluster_delta.astype(f32) * cluster_weight.astype(f32).T
 
+    deltas = jnp.concatenate([head_delta, cluster_delta], axis=1)
+    deltas = jnp.pad(deltas, ((0, 0), (0, -deltas.shape[1] % 128)))
+    deltas, behind, logit_parts = lax.optimization_barrier((deltas, rows_hidden, logit_parts))
+    deltas = jnp.concatenate(gather_turned(deltas, "dp"))
+    pieces = behind.reshape(span, n_dp, share).transpose(1, 0, 2).reshape(n_dp * span, share)
+    hidden_columns = jnp.concatenate(scatter_turned(pieces, "dp"))
+
+    word_logits = functools.reduce(jnp.add, logit_parts)
     word_top = jnp.max(word_logits, axis=1, keepdims=True)
     word_exp = jnp.exp(word_logits - word_top)
     word_prob = word_exp / jnp.sum(word_exp, axis=1, keepdims=True)
     word_columns = jnp.arange(word_logits.shape[1], dtype=jnp.int32)
     word_hot = (word_columns[None, :] == own_words[:, None]).astype(f32)
     own_word_delta = (own_gains[:, None] * (word_prob - word_hot)).astype(bf16)
-    deltas = jnp.concatenate([head_delta, cluster_delta], axis=1)
-    deltas = jnp.pad(deltas, ((0, 0), (0, -deltas.shape[1] % 128)))
-    word_delta, deltas = exchange("dp", [own_word_delta, deltas], [], 4)
+    (word_delta,) = exchange("dp", [own_word_delta], [], 4)
     word_delta = word_delta.reshape(n_dp * cap, -1)
-    deltas = deltas.reshape(n_dp * span, -1)
     all_delta, all_cluster_delta = deltas[:, :width], deltas[:, width : width + 1]
     reduced_grad = lax.dot_general(
         word_delta, out, (((1,), (1,)), ((), ())), preferred_element_type=f32
@@ -260,8 +284,8 @@
     tail_partial = lax.dot_general(
         reduced_grad, proj, (((1,), (1,)), ((), ())), preferred_element_type=f32
     )
-    (tail_parts,) = exchange("dp", [], [tail_partial.astype(bf16).reshape(n_dp, cap, model)], 5)
-    tail_sum = jnp.sum(tail_parts.astype(f32), axis=0).astype(bf16)
+    tail_parts = scatter_turned(tail_partial.astype(bf16), "dp")
+    tail_sum = functools.reduce(jnp.add, [part.astype(f32) for part in tail_parts]).astype(bf16)
     out_grad = lax.dot_general(
         reduced, word_delta, (((0,), (0,)), ((), ())), preferred_element_type=f32
     ).astype(bf16)
@@ -279,8 +303,8 @@
     spread_back = lax.dot_general(
         own_select.astype(bf16), tail_sum, (((0,), (0,)), ((), ())), preferred_element_type=f32
     )
-    partial = (token_partial + spread_back).reshape(n_vocab, local, model)
-    hidden_grad = pair_scatter("vocab", partial, 6).astype(bf16)
+    partial = (token_partial + spread_back).reshape(n_vocab, 2 * local, model // 2)
+    hidden_grad = pair_scatter("vocab", partial, 6).reshape(local, model).astype(bf16)
     return (hidden_grad, head_grad, cluster_grad, proj_grad[None], out_grad[None])
 
 

time: 167 us -> 139 us (0.83)
  Pallas kernels: 88.5 us -> 58.1 us
  starting transfers between devices: 0.04 us -> 15.2 us
  between operations: 14.2 us -> 0.96 us
  local copies, waits for them, and re-layouts: 7.57 us -> 18.3 us
  waiting for transfers between devices: 9.84 us -> 2.28 us
  other arithmetic: 12.3 us -> 9.18 us
    pallas_call x6 -> x5, Pallas kernels: 88.5 us -> 58.1 us  [call(): pl.pallas_call(body, out_shape=results, in_specs=[vmem] * len(operands),...]
    ppermute x0 -> x12, starting transfers between devices: none -> 15.2 us  [the longest x9 11.4 us: scatter_turned(): lax.ppermute(part(k), axis, turned(axis, k))]
    reduce_scatter x1 -> x0, waiting for transfers between devices: 9.82 us -> none  [shards(): lax.psum_scatter(partial_logits, 'dp', scatter_dimension=0, tiled=True)]
    dynamic_slice x0 -> x3, local copies, waits for them, and re-layouts: none -> 4.22 us  [part(): return lax.dynamic_slice_in_dim(x, lax.rem(me + k, n) * rows, rows, 0)]
    unnamed x12 -> x21, local copies, waits for them, and re-layouts: 0.03 us -> 3.99 us
    another operation x2 -> x1, local copies, waits for them, and re-layouts: 2.34 us -> 0.01 us  [shards(): pieces = rows_hidden.reshape(span, n_dp, share).transpose(1, 0, 2)]
    ppermute x0 -> x12, waiting for transfers between devices: none -> 2.28 us  [the longest x9 2.27 us: scatter_turned(): lax.ppermute(part(k), axis, turned(axis, k))]
  transfers between devices with their start and end apart: 1 -> 12, of which waited for: 1 -> 1; matrix products, arithmetic and copies ran while one was open for 11% -> 31% of each run, Pallas kernels for 4% -> 23%
where the time goes in v3:
time: 139 us; the launch traced here: 138 us
  Pallas kernels  58.1 us (42%)
  matrix products  34 us (24%)
  local copies, waits for them, and re-layouts  18.3 us (13%)
  starting transfers between devices  15.2 us (11%)
  other arithmetic  9.18 us (7%)
  waiting for transfers between devices  2.28 us (2%)
    pallas_call x5, Pallas kernels, call(): pl.pallas_call(body, out_shape=results, in_specs=[vmem] * len(operands),...  58.1 us
    ppermute x9, starting transfers between devices, scatter_turned(): lax.ppermute(part(k), axis, turned(axis, k))  11.4 us
    dot_general x1, matrix products, shards(): lax.dot_general(head_delta, head_weight, (((1,), (1,)), ((), ())), prefer...  8.22 us
    dot_general x1, matrix products, shards(): local_logits = jnp.dot(rows_hidden, head_weight, preferred_element_type=f32)  5.99 us
    dynamic_slice x3, local copies, waits for them, and re-layouts, part(): return lax.dynamic_slice_in_dim(x, lax.rem(me + k, n) * rows, rows, 0)  4.22 us
    unnamed x21, local copies, waits for them, and re-layouts  3.99 us
    ppermute x3, starting transfers between devices, gather_turned(): lax.ppermute(x, axis, turned(axis, k))  3.87 us
    dot_general x1, matrix products, shards(): lax.dot_general(hidden_columns, all_delta, (((0,), (0,)), ((), ())), pref...  3.62 us
  transfers between devices with their start and end apart: 12, of which 1 were waited for; matrix products, arithmetic and copies ran while one was open for 31% of the time, Pallas kernels for 23%

profile of v3, /device:TPU:0, one launch (start us, length us, event | category | flops | bytes accessed | tf_op | source)
XLA Modules:
  0.0 138.0 jit_solution(9697378876027713260)
XLA Ops:
  2.1 1.5 %reshape.116.refs_0_ = bf16[16,2048]{1,0:T(8,128)(2,1)} reshape(bf16[8,4096]{1,0:T(8,128)(2,1)} %param.7) | data formatting | bytes 131072 | tf_op jit(solution)/shard_map/reshape | solution.py:214
  4.2 14.8 %shard_map.110 = (bf16[8,16,2048]{2,1,0:T(8,128)(2,1)}, f32[8,8,128]{2,1,0:T(8,128)}) custom-call(bf16[16,2048]{1,0:T(8,128)(2,1)} %reshape.116.refs_0_, f32[8,128]{1,0:T(8,128)} %select_maximum_fusion.1.refs_1_), custom_call_target="tpu_custom_call" | custom-call | tf_op jit(solution)/shard_map/pallas_call | solution.py:33
  19.0 1.2 reshape.117
  22.1 11.6 %shard_map.111 = bf16[4,16,4096]{2,1,0:T(8,128)(2,1)} custom-call(bf16[16,4096]{1,0:T(8,128)(2,1)} %convolution_convert_fusion.3.refs_0_), custom_call_target="tpu_custom_call" | custom-call | tf_op jit(solution)/shard_map/pallas_call | solution.py:33
  33.7 1.5 %fusion.12 = bf16[64,256]{1,0:T(8,128)(2,1)S(1)} fusion(bf16[64,4096]{1,0:T(8,128)(2,1)} %bitcast.58, bf16[1,4096,256]{2,1,0:T(8,128)(2,1)S(1)} %copy-done), kind=kOutput, calls=%fused_computation.17 | convolution fusion | flops 134234112 | bytes 2654208 | tf_op jit(solution)/shard_map/dot_general | solution.py:234
  35.2 2.1 %fusion.4 = f32[64,7680]{1,0:T(8,128)} fusion(bf16[64,256]{1,0:T(8,128)(2,1)S(1)} %fusion.12, bf16[1,256,7680]{2,1,0:T(8,128)(2,1)S(1)} %copy-done.1), kind=kOutput, calls=%fused_computation.10 | convolution fusion | flops 251658240 | bytes 5931008 | tf_op jit(solution)/shard_map/dot_general | solution.py:235
  37.3 2.6 %constant_dynamic-slice_fusion.7 = (f32[16,7680]{1,0:T(8,128)}, f32[16,7680]{1,0:T(8,128)}, f32[16,7680]{1,0:T(8,128)}, f32[16,7680]{1,0:T(8,128)S(1)}) fusion(f32[64,7680]{1,0:T(8,128)} %fusion.4, s32[]{:T(128)S(6)} %select_n.75, s32[]{:T(128)S(6)} %select_n.74, s32[]{:T(128)S(6)} %select_n.73, s32[]{:T(128)S(6)} %select_n.72), kind=kLoop, calls=%fused_computation.68 | loop fusion | bytes 3932176 | tf_op jit(solution)/shard_map/dynamic_slice | solution.py:193
  39.9 2.3 %collective-permute-start.2 = (f32[16,7680]{1,0:T(8,128)}, f32[16,7680]{1,0:T(8,128)}, u32[]{:S(2)}, u32[]{:S(2)}) collective-permute-start(f32[16,7680]{1,0:T(8,128)} %get-tuple-element.32), channel_id=1, source_target_pairs={{0,24},{8,0},{16,8},{24,16},{1,25},{9,1},{17,9},{25,17},{2,26},{10... | collective-permute-start | bytes 1474568 | tf_op jit(solution)/shard_map/ppermute | solution.py:195
  45.1 6.0 %fusion.39 = (f32[64]{0:T(128)S(1)}, f32[64,1280]{1,0:T(8,128)S(1)}) fusion(bf16[64,4096]{1,0:T(8,128)(2,1)S(1)} %reshape.117, bf16[4096,1280]{1,0:T(8,128)(2,1)} %param.10), kind=kOutput, calls=%fused_computation.90 | convolution fusion | flops 671170496 | bytes 11337984 | tf_op jit(solution)/shard_map/dot_general | solution.py:240
  52.2 6.9 %shard_map.112 = f32[8,8,128]{2,1,0:T(8,128)} custom-call(f32[8,128]{1,0:T(8,128)} %select_maximum_fusion.refs_0_), custom_call_target="tpu_custom_call" | custom-call | tf_op jit(solution)/shard_map/pallas_call | solution.py:33
  60.9 8.2 %convolution_add_fusion.1 = f32[64,4096]{1,0:T(8,128)} fusion(bf16[64,1280]{1,0:T(8,128)(2,1)S(1)} %multiply_convert_fusion.1, bf16[4096,1280]{1,0:T(8,128)(2,1)} %param.10, f32[4096]{0:T(1024)S(1)} %mul.79, f32[64]{0:T(128)S(1)} %get-tuple-element.27), kind=kOutput, calls=%fused_computation.5 | convolution fusion | flops 671612928 | bytes 11714816 | tf_op jit(solution)/shard_map/dot_general | solution.py:260
  69.2 2.4 %collective-permute-start.11 = (bf16[64,1408]{1,0:T(8,128)(2,1)}, bf16[64,1408]{1,0:T(8,128)(2,1)}, u32[]{:S(2)}, u32[]{:S(2)}) collective-permute-start(bf16[64,1408]{1,0:T(8,128)(2,1)} %fusion.19), channel_id=1, source_target_pairs={{0,24},{8,0},{16,8},{24,16},{1,25},{9,1},{17,9},{25,17},{2,26},{10... | collective-permute-start | bytes 540680 | tf_op jit(solution)/shard_map/ppermute | solution.py:185
  71.6 1.5 %collective-permute-start.10 = (bf16[64,1408]{1,0:T(8,128)(2,1)}, bf16[64,1408]{1,0:T(8,128)(2,1)}, u32[]{:S(2)}, u32[]{:S(2)}) collective-permute-start(bf16[64,1408]{1,0:T(8,128)(2,1)} %fusion.19), channel_id=1, source_target_pairs={{0,16},{8,24},{16,0},{24,8},{1,17},{9,25},{17,1},{25,9},{2,18},{10... | collective-permute-start | bytes 540680 | tf_op jit(solution)/shard_map/ppermute | solution.py:185
  73.1 1.6 %constant_dynamic-update-slice_fusion.3 = bf16[256,1408]{1,0:T(8,128)(2,1)} fusion(bf16[64,1408]{1,0:T(8,128)(2,1)} %fusion.19), kind=kLoop, calls=%fused_computation.42 | loop fusion | bytes 360448
  74.7 1.5 %fusion.35 = (f32[16]{0:T(128)S(1)}, f32[16,7680]{1,0:T(8,128)S(1)}) fusion(f32[16,7680]{1,0:T(8,128)} %collective-permute-done.2, f32[16,7680]{1,0:T(8,128)} %collective-permute-done.1, f32[16,7680]{1,0:T(8,128)S(1)} %get-tuple-element.19, f32[16,7680]{1,0:T(8,128)} %collective-permute-done), kind=kLoop, calls=%fused_computation.87 | loop fusion | flops 491504 | bytes 2457664 | tf_op jit(solution)/shard_map/reduce_max | solution.py:272
  77.4 14.7 %shard_map.113 = bf16[4,16,7680]{2,1,0:T(8,128)(2,1)} custom-call(bf16[16,7680]{1,0:T(8,128)(2,1)} %multiply_convert_fusion.refs_0_), custom_call_target="tpu_custom_call" | custom-call | tf_op jit(solution)/shard_map/pallas_call | solution.py:33
  92.1 2.6 %fusion.9 = bf16[64,256]{1,0:T(8,128)(2,1)S(1)} fusion(bf16[64,7680]{1,0:T(8,128)(2,1)} %bitcast.56, bf16[1,256,7680]{2,1,0:T(8,128)(2,1)S(1)} %copy-done.2), kind=kOutput, calls=%fused_computation.16 | convolution fusion | flops 251674624 | bytes 4947968 | tf_op jit(solution)/shard_map/dot_general | solution.py:281
  94.7 3.1 %fusion = bf16[1,256,7680]{2,1,0:T(8,128)(2,1)} fusion(bf16[64,256]{1,0:T(8,128)(2,1)S(1)} %fusion.12, bf16[64,7680]{1,0:T(8,128)(2,1)S(1)} %bitcast.57), kind=kOutput, calls=%fused_computation.1 | convolution fusion | flops 253624320 | bytes 4947968 | tf_op jit(solution)/shard_map/dot_general | solution.py:289
  99.4 1.8 %collective-permute-start.3 = (bf16[16,4096]{1,0:T(8,128)(2,1)S(1)}, bf16[16,4096]{1,0:T(8,128)(2,1)}, u32[]{:S(2)}, u32[]{:S(2)}) collective-permute-start(bf16[16,4096]{1,0:T(8,128)(2,1)S(1)} %get-tuple-element.40), channel_id=1, source_target_pairs={{0,8},{8,16},{16,24},{24,0},{1,9},{9,17},{17,25},{25,1},{2,10},{10... | collective-permute-start | bytes 393224 | tf_op jit(solution)/shard_map/ppermute | solution.py:195
  101.1 1.2 collective-permute-start.5
  102.3 1.5 %collective-permute-start.4 = (bf16[16,4096]{1,0:T(8,128)(2,1)S(1)}, bf16[16,4096]{1,0:T(8,128)(2,1)}, u32[]{:S(2)}, u32[]{:S(2)}) collective-permute-start(bf16[16,4096]{1,0:T(8,128)(2,1)S(1)} %get-tuple-element.42), channel_id=1, source_target_pairs={{0,16},{8,24},{16,0},{24,8},{1,17},{9,25},{17,1},{25,9},{2,18},{10... | collective-permute-start | bytes 393224 | tf_op jit(solution)/shard_map/ppermute | solution.py:195
  103.8 2.1 %fusion.1 = bf16[1,4096,256]{2,1,0:T(8,128)(2,1)} fusion(bf16[64,4096]{1,0:T(8,128)(2,1)S(1)} %bitcast.59, bf16[64,256]{1,0:T(8,128)(2,1)S(1)} %fusion.9), kind=kOutput, calls=%fused_computation.3 | convolution fusion | flops 135266304 | bytes 2654208 | tf_op jit(solution)/shard_map/dot_general | solution.py:292
  107.3 2.9 %collective-permute-start.8 = (bf16[64,1024]{1,0:T(8,128)(2,1)}, bf16[64,1024]{1,0:T(8,128)(2,1)}, u32[]{:S(2)}, u32[]{:S(2)}) collective-permute-start(bf16[64,1024]{1,0:T(8,128)(2,1)} %get-tuple-element.37), channel_id=1, source_target_pairs={{0,24},{8,0},{16,8},{24,16},{1,25},{9,1},{17,9},{25,17},{2,26},{10... | collective-permute-start | bytes 393224 | tf_op jit(solution)/shard_map/ppermute | solution.py:195
  110.7 1.8 %convolution_add_fusion = f32[64,4096]{1,0:T(8,128)S(1)} fusion(f32[64,4096]{1,0:T(8,128)} %convolution_add_fusion.1, bf16[16,4096]{1,0:T(8,128)(2,1)} %collective-permute-done.5, bf16[16,4096]{1,0:T(8,128)(2,1)} %collective-permute-done.4, bf16[16,4096]{1,0:T(8,128)(2,1)} %collective-permute-done.3, bf16[64,4096]{1,0:T(8,128)(2,1)} %copy-done.5, ...), kind=kOutput, calls=%fused_computation.4 | convolution fusion | flops 9177088 | bytes 2621764 | tf_op jit(solution)/shard_map/dot_general | solution.py:303
  112.6 1.1 reshape.121.x
  113.7 10.2 %shard_map.114 = f32[16,2048]{1,0:T(8,128)} custom-call(f32[8,16,2048]{2,1,0:T(8,128)} %reshape.121.x), custom_call_target="tpu_custom_call" | custom-call | tf_op jit(solution)/shard_map/pallas_call | solution.py:33
  126.2 1.6 %constant_dynamic-update-slice_fusion.1 = bf16[256,1408]{1,0:T(8,128)(2,1)} fusion(bf16[256,1408]{1,0:T(8,128)(2,1)} %constant_dynamic-update-slice_fusion.2, bf16[64,1408]{1,0:T(8,128)(2,1)} %collective-permute-done.10), kind=kLoop, calls=%fused_computation.40 | loop fusion | bytes 360448
  127.9 1.6 %constant_dynamic-update-slice_fusion = bf16[256,1408]{1,0:T(8,128)(2,1)} fusion(bf16[256,1408]{1,0:T(8,128)(2,1)} %constant_dynamic-update-slice_fusion.1, bf16[64,1408]{1,0:T(8,128)(2,1)} %collective-permute-done.11), kind=kLoop, calls=%fused_computation.39 | loop fusion | bytes 360448 | tf_op jit(solution)/shard_map/concatenate | solution.py:267
  129.4 0.9 slice_reduce_fusion
  130.4 2.2 %collective-permute-done.6 = bf16[64,1024]{1,0:T(8,128)(2,1)S(1)} collective-permute-done((bf16[64,1024]{1,0:T(8,128)(2,1)}, bf16[64,1024]{1,0:T(8,128)(2,1)S(1)}, u32[]{:S(2)}, u32[]{:S(2)}) %collective-permute-start.6) | collective-permute-done | bytes 131104 | tf_op jit(solution)/shard_map/ppermute | solution.py:195
  132.6 1.1 fusion.21
  134.4 3.6 %convolution_convert_fusion.4 = bf16[1024,1280]{1,0:T(8,128)(2,1)} fusion(bf16[256,1408]{1,0:T(8,128)(2,1)} %constant_dynamic-update-slice_fusion, bf16[64,1024]{1,0:T(8,128)(2,1)} %collective-permute-done.8, bf16[64,1024]{1,0:T(8,128)(2,1)} %collective-permute-done.7, bf16[64,1024]{1,0:T(8,128)(2,1)S(1)} %collective-permute-done.6, ...), kind=kOutput, calls=%fused_computation.12 | convolution fusion | flops 674496512 | bytes 3801088 | tf_op jit(solution)/shard_map/dot_general | solution.py:296
  (74 shorter events, 17.4 us)
Async XLA Ops:
  0.6 33.0 %copy-start = (bf16[1,4096,256]{2,1,0:T(8,128)(2,1)S(1)}, bf16[1,4096,256]{2,1,0:T(8,128)(2,1)}, u32[]{:S(2)}) copy-start(bf16[1,4096,256]{2,1,0:T(8,128)(2,1)} %param.12) | copy-start | bytes 6291460
  21.1 14.1 %copy-start.1 = (bf16[1,256,7680]{2,1,0:T(8,128)(2,1)S(1)}, bf16[1,256,7680]{2,1,0:T(8,128)(2,1)}, u32[]{:S(2)}) copy-start(bf16[1,256,7680]{2,1,0:T(8,128)(2,1)} %param.13) | copy-start | bytes 11796484
  35.2 9.0 %copy-start.7 = (bf16[4096,1]{0,1:T(2,128)(2,1)S(1)}, bf16[4096,1]{0,1:T(2,128)(2,1)}, u32[]{:S(2)}) copy-start(bf16[4096,1]{0,1:T(2,128)(2,1)} %param.11) | copy-start | bytes 24580
  39.9 29.3 %collective-permute-start.2 = (f32[16,7680]{1,0:T(8,128)}, f32[16,7680]{1,0:T(8,128)}, u32[]{:S(2)}, u32[]{:S(2)}) collective-permute-start(f32[16,7680]{1,0:T(8,128)} %get-tuple-element.32), channel_id=1, source_target_pairs={{0,24},{8,0},{16,8},{24,16},{1,25},{9,1},{17,9},{25,17},{2,26},{10... | collective-permute-start | bytes 1474568 | tf_op jit(solution)/shard_map/ppermute | solution.py:195
  42.2 26.9 %collective-permute-start.1 = (f32[16,7680]{1,0:T(8,128)}, f32[16,7680]{1,0:T(8,128)}, u32[]{:S(2)}, u32[]{:S(2)}) collective-permute-start(f32[16,7680]{1,0:T(8,128)} %get-tuple-element.33), channel_id=1, source_target_pairs={{0,16},{8,24},{16,0},{24,8},{1,17},{9,25},{17,1},{25,9},{2,18},{10... | collective-permute-start | bytes 1474568 | tf_op jit(solution)/shard_map/ppermute | solution.py:195
  42.8 26.4 %collective-permute-start = (f32[16,7680]{1,0:T(8,128)}, f32[16,7680]{1,0:T(8,128)}, u32[]{:S(2)}, u32[]{:S(2)}) collective-permute-start(f32[16,7680]{1,0:T(8,128)} %get-tuple-element.34), channel_id=1, source_target_pairs={{0,8},{8,16},{16,24},{24,0},{1,9},{9,17},{17,25},{25,1},{2,10},{10... | collective-permute-start | bytes 1474568 | tf_op jit(solution)/shard_map/ppermute | solution.py:195
  60.9 15.6 %copy-start.8 = (f32[16]{0:T(128)S(1)}, f32[16]{0:T(128)}, u32[]{:S(2)}) copy-start(f32[16]{0:T(128)} %select_reduce_fusion.1) | copy-start | bytes 196
  69.2 23.0 %copy-start.2 = (bf16[1,256,7680]{2,1,0:T(8,128)(2,1)S(1)}, bf16[1,256,7680]{2,1,0:T(8,128)(2,1)}, u32[]{:S(2)}) copy-start(bf16[1,256,7680]{2,1,0:T(8,128)(2,1)} %param.13) | copy-start | bytes 11796484
  69.2 58.7 %collective-permute-start.11 = (bf16[64,1408]{1,0:T(8,128)(2,1)}, bf16[64,1408]{1,0:T(8,128)(2,1)}, u32[]{:S(2)}, u32[]{:S(2)}) collective-permute-start(bf16[64,1408]{1,0:T(8,128)(2,1)} %fusion.19), channel_id=1, source_target_pairs={{0,24},{8,0},{16,8},{24,16},{1,25},{9,1},{17,9},{25,17},{2,26},{10... | collective-permute-start | bytes 540680 | tf_op jit(solution)/shard_map/ppermute | solution.py:185
  71.6 54.6 %collective-permute-start.10 = (bf16[64,1408]{1,0:T(8,128)(2,1)}, bf16[64,1408]{1,0:T(8,128)(2,1)}, u32[]{:S(2)}, u32[]{:S(2)}) collective-permute-start(bf16[64,1408]{1,0:T(8,128)(2,1)} %fusion.19), channel_id=1, source_target_pairs={{0,16},{8,24},{16,0},{24,8},{1,17},{9,25},{17,1},{25,9},{2,18},{10... | collective-permute-start | bytes 540680 | tf_op jit(solution)/shard_map/ppermute | solution.py:185
  92.1 2.6 %copy-start.3 = (bf16[4,16,7680]{2,1,0:T(8,128)(2,1)S(1)}, bf16[4,16,7680]{2,1,0:T(8,128)(2,1)}, u32[]{:S(2)}) copy-start(bf16[4,16,7680]{2,1,0:T(8,128)(2,1)} %shard_map.113) | copy-start | bytes 2949124
  94.7 9.0 %copy-start.4 = (bf16[4,16,4096]{2,1,0:T(8,128)(2,1)S(1)}, bf16[4,16,4096]{2,1,0:T(8,128)(2,1)}, u32[]{:S(2)}) copy-start(bf16[4,16,4096]{2,1,0:T(8,128)(2,1)} %shard_map.111) | copy-start | bytes 1572868
  98.6 5.1 %copy-start.5 = (bf16[64,4096]{1,0:T(8,128)(2,1)}, bf16[64,4096]{1,0:T(8,128)(2,1)S(1)}, u32[]{:S(2)}) copy-start(bf16[64,4096]{1,0:T(8,128)(2,1)S(1)} %convolution_convert_fusion.2) | copy-start | bytes 1572868
  99.4 7.8 %collective-permute-start.3 = (bf16[16,4096]{1,0:T(8,128)(2,1)S(1)}, bf16[16,4096]{1,0:T(8,128)(2,1)}, u32[]{:S(2)}, u32[]{:S(2)}) collective-permute-start(bf16[16,4096]{1,0:T(8,128)(2,1)S(1)} %get-tuple-element.40), channel_id=1, source_target_pairs={{0,8},{8,16},{16,24},{24,0},{1,9},{9,17},{17,25},{25,1},{2,10},{10... | collective-permute-start | bytes 393224 | tf_op jit(solution)/shard_map/ppermute | solution.py:195
  101.1 6.1 %collective-permute-start.5 = (bf16[16,4096]{1,0:T(8,128)(2,1)}, bf16[16,4096]{1,0:T(8,128)(2,1)}, u32[]{:S(2)}, u32[]{:S(2)}) collective-permute-start(bf16[16,4096]{1,0:T(8,128)(2,1)} %get-tuple-element.41), channel_id=1, source_target_pairs={{0,24},{8,0},{16,8},{24,16},{1,25},{9,1},{17,9},{25,17},{2,26},{10... | collective-permute-start | bytes 393224 | tf_op jit(solution)/shard_map/ppermute | solution.py:195
  102.3 7.9 %collective-permute-start.4 = (bf16[16,4096]{1,0:T(8,128)(2,1)S(1)}, bf16[16,4096]{1,0:T(8,128)(2,1)}, u32[]{:S(2)}, u32[]{:S(2)}) collective-permute-start(bf16[16,4096]{1,0:T(8,128)(2,1)S(1)} %get-tuple-element.42), channel_id=1, source_target_pairs={{0,16},{8,24},{16,0},{24,8},{1,17},{9,25},{17,1},{25,9},{2,18},{10... | collective-permute-start | bytes 393224 | tf_op jit(solution)/shard_map/ppermute | solution.py:195
  107.2 18.2 %collective-permute-start.9 = (bf16[64,1408]{1,0:T(8,128)(2,1)}, bf16[64,1408]{1,0:T(8,128)(2,1)S(1)}, u32[]{:S(2)}, u32[]{:S(2)}) collective-permute-start(bf16[64,1408]{1,0:T(8,128)(2,1)} %fusion.19), channel_id=1, source_target_pairs={{0,8},{8,16},{16,24},{24,0},{1,9},{9,17},{17,25},{25,1},{2,10},{10... | collective-permute-start | bytes 540680 | tf_op jit(solution)/shard_map/ppermute | solution.py:185
  107.3 23.2 %collective-permute-start.8 = (bf16[64,1024]{1,0:T(8,128)(2,1)}, bf16[64,1024]{1,0:T(8,128)(2,1)}, u32[]{:S(2)}, u32[]{:S(2)}) collective-permute-start(bf16[64,1024]{1,0:T(8,128)(2,1)} %get-tuple-element.37), channel_id=1, source_target_pairs={{0,24},{8,0},{16,8},{24,16},{1,25},{9,1},{17,9},{25,17},{2,26},{10... | collective-permute-start | bytes 393224 | tf_op jit(solution)/shard_map/ppermute | solution.py:195
  110.1 22.5 %copy-start.6 = (bf16[64,1024]{1,0:T(8,128)(2,1)S(1)}, bf16[64,1024]{1,0:T(8,128)(2,1)}, u32[]{:S(2)}) copy-start(bf16[64,1024]{1,0:T(8,128)(2,1)} %get-tuple-element.36) | copy-start | bytes 393220
  110.1 20.3 %collective-permute-start.7 = (bf16[64,1024]{1,0:T(8,128)(2,1)}, bf16[64,1024]{1,0:T(8,128)(2,1)}, u32[]{:S(2)}, u32[]{:S(2)}) collective-permute-start(bf16[64,1024]{1,0:T(8,128)(2,1)} %get-tuple-element.38), channel_id=1, source_target_pairs={{0,16},{8,24},{16,0},{24,8},{1,17},{9,25},{17,1},{25,9},{2,18},{10... | collective-permute-start | bytes 393224 | tf_op jit(solution)/shard_map/ppermute | solution.py:195
  125.5 7.2 %collective-permute-start.6 = (bf16[64,1024]{1,0:T(8,128)(2,1)}, bf16[64,1024]{1,0:T(8,128)(2,1)S(1)}, u32[]{:S(2)}, u32[]{:S(2)}) collective-permute-start(bf16[64,1024]{1,0:T(8,128)(2,1)} %get-tuple-element.39), channel_id=1, source_target_pairs={{0,8},{8,16},{16,24},{24,0},{1,9},{9,17},{17,25},{25,1},{2,10},{10... | collective-permute-start | bytes 393224 | tf_op jit(solution)/shard_map/ppermute | solution.py:195

commit v4 on v3

--- a/solution.py
+++ b/solution.py
@@ -21,11 +21,12 @@
     )
 
 
-def greet(axis, peers):
+def greet(*groups):
     barrier = pltpu.get_barrier_semaphore()
-    for peer in peers:
-        pl.semaphore_signal(barrier, inc=1, device_id={axis: peer}, device_id_type=MESH)
-    pl.semaphore_wait(barrier, len(peers))
+    for axis, peers in groups:
+        for peer in peers:
+            pl.semaphore_signal(barrier, inc=1, device_id={axis: peer}, device_id_type=MESH)
+    pl.semaphore_wait(barrier, sum(len(peers) for _, peers in groups))
 
 
 def call(body, operands, results, scratch, collective_id):
@@ -47,7 +48,7 @@
     send, recv, local = refs[2 * count :]
     me = lax.axis_index(axis)
     peers = [lax.rem(me + k, n) for k in range(1, n)]
-    greet(axis, peers)
+    greet((axis, peers))
     copies = []
     for i in range(count):
         for k, peer in enumerate(peers):
@@ -88,7 +89,7 @@
     place, core = me // 2, lax.rem(me, 2)
     partner = 2 * place + 1 - core
     peers = [2 * lax.rem(place + k, half) + core for k in range(1, half)]
-    greet(axis, peers + [partner])
+    greet((axis, peers + [partner]))
     copies, passed = [], []
     for i in range(count):
         for k, peer in enumerate(peers):
@@ -129,19 +130,35 @@
     )
 
 
-def pair_scatter_body(axis, n, x, out, theirs, leaving, landed, send, recv, pair_send, pair_recv):
+def pair_scatter_body(
+    axis, n, other, m, x, whole, parts, out, wholes, gathered,
+    theirs, leaving, landed, send, recv, pair_send, pair_recv, far_send, far_recv, local,
+):
+    here = lax.axis_index(other)
+    far = [lax.rem(here + k, m) for k in range(1, m)]
     half = n // 2
     me = lax.axis_index(axis)
     place, core = me // 2, lax.rem(me, 2)
     partner = 2 * place + 1 - core
     order = [lax.rem(place + k, half) for k in range(1, half)]
-    greet(axis, [2 * p + core for p in order] + [partner])
+    greet((axis, [2 * p + core for p in order] + [partner]), (other, far))
     order = order + [place]
-    pairs, copies = [], []
+    pairs, copies, crossing = [], [], []
     for k, p in enumerate(order):
         copy = remote(x.at[2 * p + 1 - core], theirs.at[k], pair_send.at[k], pair_recv.at[k], axis, partner)
         copy.start()
         pairs.append(copy)
+    for k, peer in enumerate(far):
+        crossing += [
+            remote(whole, wholes.at[here], far_send.at[0, k], far_recv.at[0, k], other, peer),
+            remote(parts.at[peer], gathered.at[here], far_send.at[1, k], far_recv.at[1, k], other, peer),
+        ]
+    crossing += [
+        pltpu.make_async_copy(whole, wholes.at[here], local.at[0]),
+        pltpu.make_async_copy(parts.at[here], gathered.at[here], local.at[1]),
+    ]
+    for copy in crossing:
+        copy.start()
     for k, p in enumerate(order):
         pairs[k].wait_recv()
         total = x[2 * p + core] + theirs[k]
@@ -156,33 +173,37 @@
     out[...] = total
     for copy in pairs + copies:
         copy.wait_send()
-
-
-def pair_scatter(axis, x, collective_id):
-    n = lax.axis_size(axis)
+    for copy in crossing:
+        copy.wait()
+
+
+def pair_scatter(axis, x, other, whole, parts, collective_id):
+    n, m = lax.axis_size(axis), lax.axis_size(other)
     half = n // 2
     block = x.shape[1:]
     dma = pltpu.SemaphoreType.DMA
     return call(
-        functools.partial(pair_scatter_body, axis, n),
-        [x], [jax.ShapeDtypeStruct(block, x.dtype)],
+        functools.partial(pair_scatter_body, axis, n, other, m),
+        [x, whole, parts],
+        [
+            jax.ShapeDtypeStruct(block, x.dtype),
+            jax.ShapeDtypeStruct((m, *whole.shape), whole.dtype),
+            jax.ShapeDtypeStruct(parts.shape, parts.dtype),
+        ],
         [
             pltpu.VMEM((half, *block), x.dtype),
             pltpu.VMEM((half - 1, *block), jnp.bfloat16),
             pltpu.VMEM((half - 1, *block), jnp.bfloat16),
             dma((half - 1,)), dma((half - 1,)), dma((half,)), dma((half,)),
+            dma((2, m - 1)), dma((2, m - 1)), dma((2,)),
         ],
         collective_id,
-    )[0]
+    )
 
 
 def turned(axis, k):
     n = lax.axis_size(axis)
     return [(i, (i + k) % n) for i in range(n)]
-
-
-def gather_turned(x, axis):
-    return [x] + [lax.ppermute(x, axis, turned(axis, k)) for k in range(1, lax.axis_size(axis))]
 
 
 def scatter_turned(x, axis):
@@ -263,10 +284,8 @@
 
     deltas = jnp.concatenate([head_delta, cluster_delta], axis=1)
     deltas = jnp.pad(deltas, ((0, 0), (0, -deltas.shape[1] % 128)))
-    deltas, behind, logit_parts = lax.optimization_barrier((deltas, rows_hidden, logit_parts))
-    deltas = jnp.concatenate(gather_turned(deltas, "dp"))
-    pieces = behind.reshape(span, n_dp, share).transpose(1, 0, 2).reshape(n_dp * span, share)
-    hidden_columns = jnp.concatenate(scatter_turned(pieces, "dp"))
+    deltas, token_partial, logit_parts = lax.optimization_barrier((deltas, token_partial, logit_parts))
+    pieces = rows_hidden.reshape(span, n_dp, share).transpose(1, 0, 2)
 
     word_logits = functools.reduce(jnp.add, logit_parts)
     word_top = jnp.max(word_logits, axis=1, keepdims=True)
@@ -277,7 +296,6 @@
     own_word_delta = (own_gains[:, None] * (word_prob - word_hot)).astype(bf16)
     (word_delta,) = exchange("dp", [own_word_delta], [], 4)
     word_delta = word_delta.reshape(n_dp * cap, -1)
-    all_delta, all_cluster_delta = deltas[:, :width], deltas[:, width : width + 1]
     reduced_grad = lax.dot_general(
         word_delta, out, (((1,), (1,)), ((), ())), preferred_element_type=f32
     ).astype(bf16)
@@ -293,18 +311,22 @@
         tail_rows, reduced_grad, (((0,), (0,)), ((), ())), preferred_element_type=f32
     ).astype(bf16)
 
+    spread_back = lax.dot_general(
+        own_select.astype(bf16), tail_sum, (((0,), (0,)), ((), ())), preferred_element_type=f32
+    )
+    partial = (token_partial + spread_back).reshape(n_vocab, 2 * local, model // 2)
+    hidden_grad, deltas, hidden_columns = pair_scatter("vocab", partial, "dp", deltas, pieces, 6)
+    hidden_grad = hidden_grad.reshape(local, model).astype(bf16)
+    deltas = deltas.reshape(n_dp * span, -1)
+    hidden_columns = hidden_columns.reshape(n_dp * span, share)
+    all_delta, all_cluster_delta = deltas[:, :width], deltas[:, width : width + 1]
+
     head_grad = lax.dot_general(
         hidden_columns, all_delta, (((0,), (0,)), ((), ())), preferred_element_type=f32
     ).astype(bf16)
     cluster_grad = lax.dot_general(
         hidden_columns, all_cluster_delta, (((0,), (0,)), ((), ())), preferred_element_type=f32
     ).astype(bf16)
-
-    spread_back = lax.dot_general(
-        own_select.astype(bf16), tail_sum, (((0,), (0,)), ((), ())), preferred_element_type=f32
-    )
-    partial = (token_partial + spread_back).reshape(n_vocab, 2 * local, model // 2)
-    hidden_grad = pair_scatter("vocab", partial, 6).reshape(local, model).astype(bf16)
     return (hidden_grad, head_grad, cluster_grad, proj_grad[None], out_grad[None])
 
 

time: 139 us -> 134 us (0.964)
  Pallas kernels: 58.1 us -> 68 us
  local copies, waits for them, and re-layouts: 18.3 us -> 10.7 us
  starting transfers between devices: 15.2 us -> 8.74 us
  matrix products: 34 us -> 31.7 us
  other arithmetic: 9.18 us -> 10.7 us
    pallas_call x5, Pallas kernels: 58.1 us -> 68 us  [call(): pl.pallas_call(body, out_shape=results, in_specs=[vmem] * len(operands),...]
    unnamed x21 -> x16, local copies, waits for them, and re-layouts: 3.99 us -> 0.04 us
    ppermute x3 -> x0, starting transfers between devices: 3.87 us -> none  [gather_turned(): lax.ppermute(x, axis, turned(axis, k))]
    ppermute x9 -> x6, starting transfers between devices: 11.4 us -> 8.74 us  [scatter_turned(): lax.ppermute(part(k), axis, turned(axis, k))]
    concatenate x1 -> x0, local copies, waits for them, and re-layouts: 1.59 us -> none  [shards(): deltas = jnp.concatenate(gather_turned(deltas, 'dp'))]
    dynamic_slice x3 -> x2, local copies, waits for them, and re-layouts: 4.22 us -> 2.63 us  [part(): return lax.dynamic_slice_in_dim(x, lax.rem(me + k, n) * rows, rows, 0)]
    dot_general x1, matrix products: 1.84 us -> 0.35 us  [shards(): lax.dot_general(own_select.astype(bf16), tail_sum, (((0,), (0,)), ((), ()...]
  transfers between devices with their start and end apart: 12 -> 6, of which waited for: 1 -> 2; matrix products, arithmetic and copies ran while one was open for 31% -> 17% of each run, Pallas kernels for 23% -> 5%
where the time goes in v4:
time: 134 us; the launch traced here: 133 us
  Pallas kernels  68 us (51%)
  matrix products  31.7 us (24%)
  local copies, waits for them, and re-layouts  10.7 us (8%)
  other arithmetic  10.7 us (8%)
  starting transfers between devices  8.74 us (7%)
  waiting for transfers between devices  1.99 us (1%)
    pallas_call x5, Pallas kernels, call(): pl.pallas_call(body, out_shape=results, in_specs=[vmem] * len(operands),...  68 us
    ppermute x6, starting transfers between devices, scatter_turned(): lax.ppermute(part(k), axis, turned(axis, k))  8.74 us
    dot_general x1, matrix products, shards(): lax.dot_general(head_delta, head_weight, (((1,), (1,)), ((), ())), prefer...  7.24 us
    dot_general x1, matrix products, shards(): local_logits = jnp.dot(rows_hidden, head_weight, preferred_element_type=f32)  6 us
    dot_general x1, matrix products, shards(): lax.dot_general(hidden_columns, all_delta, (((0,), (0,)), ((), ())), pref...  3.65 us
    dot_general x1, matrix products, shards(): lax.dot_general(reduced, word_delta, (((0,), (0,)), ((), ())), preferred_...  3.13 us
  transfers between devices with their start and end apart: 6, of which 2 were waited for; matrix products, arithmetic and copies ran while one was open for 17% of the time, Pallas kernels for 5%

profile of v4, /device:TPU:0, one launch (start us, length us, event | category | flops | bytes accessed | tf_op | source)
XLA Modules:
  0.0 132.8 jit_solution(2308452647225950627)
XLA Ops:
  0.7 1.6 %reshape.119.refs_0_ = bf16[16,2048]{1,0:T(8,128)(2,1)} reshape(bf16[8,4096]{1,0:T(8,128)(2,1)} %param.7) | data formatting | bytes 131072 | tf_op jit(solution)/shard_map/reshape | solution.py:235
  4.2 14.8 %shard_map.110 = (bf16[8,16,2048]{2,1,0:T(8,128)(2,1)}, f32[8,8,128]{2,1,0:T(8,128)}) custom-call(bf16[16,2048]{1,0:T(8,128)(2,1)} %reshape.119.refs_0_, f32[8,128]{1,0:T(8,128)} %select_maximum_fusion.1.refs_1_), custom_call_target="tpu_custom_call" | custom-call | tf_op jit(solution)/shard_map/pallas_call | solution.py:34
  19.0 0.8 convert_reduce_fusion.1
  20.0 1.2 reshape.120
  21.2 0.8 convolution_convert_fusion.3.refs_0_
  22.1 11.7 %shard_map.111 = bf16[4,16,4096]{2,1,0:T(8,128)(2,1)} custom-call(bf16[16,4096]{1,0:T(8,128)(2,1)} %convolution_convert_fusion.3.refs_0_), custom_call_target="tpu_custom_call" | custom-call | tf_op jit(solution)/shard_map/pallas_call | solution.py:34
  33.8 1.5 %fusion.12 = bf16[64,256]{1,0:T(8,128)(2,1)S(1)} fusion(bf16[64,4096]{1,0:T(8,128)(2,1)} %bitcast.67, bf16[1,4096,256]{2,1,0:T(8,128)(2,1)S(1)} %copy-done), kind=kOutput, calls=%fused_computation.16 | convolution fusion | flops 134234112 | bytes 2654208 | tf_op jit(solution)/shard_map/dot_general | solution.py:255
  35.3 2.1 %fusion.4 = f32[64,7680]{1,0:T(8,128)} fusion(bf16[64,256]{1,0:T(8,128)(2,1)S(1)} %fusion.12, bf16[1,256,7680]{2,1,0:T(8,128)(2,1)S(1)} %copy-done.1), kind=kOutput, calls=%fused_computation.9 | convolution fusion | flops 251658240 | bytes 5931008 | tf_op jit(solution)/shard_map/dot_general | solution.py:256
  37.4 2.6 %constant_dynamic-slice_fusion.3 = (f32[16,7680]{1,0:T(8,128)}, f32[16,7680]{1,0:T(8,128)}, f32[16,7680]{1,0:T(8,128)}, f32[16,7680]{1,0:T(8,128)S(1)}) fusion(f32[64,7680]{1,0:T(8,128)} %fusion.4, s32[]{:T(128)S(6)} %select_n.62, s32[]{:T(128)S(6)} %select_n.61, s32[]{:T(128)S(6)} %select_n.60, s32[]{:T(128)S(6)} %select_n.59), kind=kLoop, calls=%fused_computation.60 | loop fusion | bytes 3932176 | tf_op jit(solution)/shard_map/dynamic_slice | solution.py:214
  40.0 1.4 %collective-permute-start = (f32[16,7680]{1,0:T(8,128)}, f32[16,7680]{1,0:T(8,128)}, u32[]{:S(2)}, u32[]{:S(2)}) collective-permute-start(f32[16,7680]{1,0:T(8,128)} %get-tuple-element.40), channel_id=1, source_target_pairs={{0,8},{8,16},{16,24},{24,0},{1,9},{9,17},{17,25},{25,1},{2,10},{10... | collective-permute-start | bytes 1474568 | tf_op jit(solution)/shard_map/ppermute | solution.py:216
  41.5 1.5 %collective-permute-start.1 = (f32[16,7680]{1,0:T(8,128)}, f32[16,7680]{1,0:T(8,128)}, u32[]{:S(2)}, u32[]{:S(2)}) collective-permute-start(f32[16,7680]{1,0:T(8,128)} %get-tuple-element.39), channel_id=1, source_target_pairs={{0,16},{8,24},{16,0},{24,8},{1,17},{9,25},{17,1},{25,9},{2,18},{10... | collective-permute-start | bytes 1474568 | tf_op jit(solution)/shard_map/ppermute | solution.py:216
  42.9 1.5 %collective-permute-start.2 = (f32[16,7680]{1,0:T(8,128)}, f32[16,7680]{1,0:T(8,128)}, u32[]{:S(2)}, u32[]{:S(2)}) collective-permute-start(f32[16,7680]{1,0:T(8,128)} %get-tuple-element.38), channel_id=1, source_target_pairs={{0,24},{8,0},{16,8},{24,16},{1,25},{9,1},{17,9},{25,17},{2,26},{10... | collective-permute-start | bytes 1474568 | tf_op jit(solution)/shard_map/ppermute | solution.py:216
  44.4 0.8 slice_reduce_fusion
  45.7 6.0 %fusion.39 = (f32[64]{0:T(128)S(1)}, f32[64,1280]{1,0:T(8,128)S(1)}) fusion(bf16[64,4096]{1,0:T(8,128)(2,1)S(1)} %reshape.120, bf16[4096,1280]{1,0:T(8,128)(2,1)} %param.10), kind=kOutput, calls=%fused_computation.80 | convolution fusion | flops 671170496 | bytes 11337984 | tf_op jit(solution)/shard_map/dot_general | solution.py:261
  52.8 6.8 %shard_map.112 = f32[8,8,128]{2,1,0:T(8,128)} custom-call(f32[8,128]{1,0:T(8,128)} %select_maximum_fusion.refs_0_), custom_call_target="tpu_custom_call" | custom-call | tf_op jit(solution)/shard_map/pallas_call | solution.py:34
  59.6 0.8 fusion.38
  62.7 0.8 copy.26
  63.6 0.8 multiply_convert_fusion.1
  65.1 7.2 %convolution_add_fusion = f32[64,4096]{1,0:T(8,128)S(1)} fusion(bf16[64,1280]{1,0:T(8,128)(2,1)S(1)} %multiply_convert_fusion.1, bf16[4096,1280]{1,0:T(8,128)(2,1)} %param.10, f32[4096]{0:T(1024)S(1)} %mul.67, f32[64]{0:T(128)S(1)} %get-tuple-element.33), kind=kOutput, calls=%fused_computation.4 | convolution fusion | flops 671612928 | bytes 11714816 | tf_op jit(solution)/shard_map/dot_general | solution.py:281
  72.4 1.7 %fusion.35 = (f32[16]{0:T(128)S(1)}, f32[16,7680]{1,0:T(8,128)S(1)}) fusion(f32[16,7680]{1,0:T(8,128)} %collective-permute-done.2, f32[16,7680]{1,0:T(8,128)} %collective-permute-done.1, f32[16,7680]{1,0:T(8,128)S(1)} %get-tuple-element.23, f32[16,7680]{1,0:T(8,128)} %collective-permute-done), kind=kLoop, calls=%fused_computation.77 | loop fusion | flops 491504 | bytes 2457664 | tf_op jit(solution)/shard_map/reduce_max | solution.py:291
  74.3 0.9 multiply_convert_fusion.refs_0_
  75.2 15.3 %shard_map.113 = bf16[4,16,7680]{2,1,0:T(8,128)(2,1)} custom-call(bf16[16,7680]{1,0:T(8,128)(2,1)} %multiply_convert_fusion.refs_0_), custom_call_target="tpu_custom_call" | custom-call | tf_op jit(solution)/shard_map/pallas_call | solution.py:34
  90.6 2.6 %fusion.9 = bf16[64,256]{1,0:T(8,128)(2,1)S(1)} fusion(bf16[64,7680]{1,0:T(8,128)(2,1)} %bitcast.65, bf16[1,256,7680]{2,1,0:T(8,128)(2,1)S(1)} %copy-done.2), kind=kOutput, calls=%fused_computation.15 | convolution fusion | flops 251674624 | bytes 4947968 | tf_op jit(solution)/shard_map/dot_general | solution.py:299
  93.2 3.1 %fusion = bf16[1,256,7680]{2,1,0:T(8,128)(2,1)} fusion(bf16[64,256]{1,0:T(8,128)(2,1)S(1)} %fusion.12, bf16[64,7680]{1,0:T(8,128)(2,1)S(1)} %bitcast.66), kind=kOutput, calls=%fused_computation.1 | convolution fusion | flops 253624320 | bytes 4947968 | tf_op jit(solution)/shard_map/dot_general | solution.py:307
  97.1 1.4 %collective-permute-start.3 = (bf16[16,4096]{1,0:T(8,128)(2,1)S(1)}, bf16[16,4096]{1,0:T(8,128)(2,1)S(1)}, u32[]{:S(2)}, u32[]{:S(2)}) collective-permute-start(bf16[16,4096]{1,0:T(8,128)(2,1)S(1)} %get-tuple-element.42), channel_id=1, source_target_pairs={{0,8},{8,16},{16,24},{24,0},{1,9},{9,17},{17,25},{25,1},{2,10},{10... | collective-permute-start | bytes 393224 | tf_op jit(solution)/shard_map/ppermute | solution.py:216
  99.1 2.4 %collective-permute-start.5 = (bf16[16,4096]{1,0:T(8,128)(2,1)S(1)}, bf16[16,4096]{1,0:T(8,128)(2,1)S(1)}, u32[]{:S(2)}, u32[]{:S(2)}) collective-permute-start(bf16[16,4096]{1,0:T(8,128)(2,1)S(1)} %get-tuple-element.43), channel_id=1, source_target_pairs={{0,24},{8,0},{16,8},{24,16},{1,25},{9,1},{17,9},{25,17},{2,26},{10... | collective-permute-start | bytes 393224 | tf_op jit(solution)/shard_map/ppermute | solution.py:216
  101.5 2.1 %fusion.1 = bf16[1,4096,256]{2,1,0:T(8,128)(2,1)} fusion(bf16[64,4096]{1,0:T(8,128)(2,1)S(1)} %bitcast.68, bf16[64,256]{1,0:T(8,128)(2,1)S(1)} %fusion.9), kind=kOutput, calls=%fused_computation.3 | convolution fusion | flops 135266304 | bytes 2654208 | tf_op jit(solution)/shard_map/dot_general | solution.py:310
  104.2 1.4 %collective-permute-done.4 = bf16[16,4096]{1,0:T(8,128)(2,1)S(1)} collective-permute-done((bf16[16,4096]{1,0:T(8,128)(2,1)S(1)}, bf16[16,4096]{1,0:T(8,128)(2,1)S(1)}, u32[]{:S(2)}, u32[]{:S(2)}) %collective-permute-start.4) | collective-permute-done | bytes 131104 | tf_op jit(solution)/shard_map/ppermute | solution.py:216
  106.0 1.1 reshape.124.x
  107.1 19.4 %shard_map.114 = (f32[16,2048]{1,0:T(8,128)}, bf16[4,64,1408]{2,1,0:T(8,128)(2,1)}, bf16[4,64,1024]{2,1,0:T(8,128)(2,1)}) custom-call(f32[8,16,2048]{2,1,0:T(8,128)} %reshape.124.x, bf16[64,1408]{1,0:T(8,128)(2,1)} %fusion.19.whole, bf16[4,64,1024]{2,1,0:T(8,128)(2,1)} %bitcast.69), custom_call_target="tpu_custom_call" | custom-call | tf_op jit(solution)/shard_map/pallas_call | solution.py:34
  126.6 1.3 fusion.22
  127.9 3.6 %convolution_convert_fusion.4 = bf16[1024,1280]{1,0:T(8,128)(2,1)} fusion(bf16[256,1024]{1,0:T(8,128)(2,1)} %bitcast.71, bf16[256,1408]{1,0:T(8,128)(2,1)} %bitcast.73), kind=kOutput, calls=%fused_computation.11 | convolution fusion | flops 672399360 | bytes 3801088 | tf_op jit(solution)/shard_map/dot_general | solution.py:324
  (53 shorter events, 10.7 us)
Async XLA Ops:
  0.6 33.2 %copy-start = (bf16[1,4096,256]{2,1,0:T(8,128)(2,1)S(1)}, bf16[1,4096,256]{2,1,0:T(8,128)(2,1)}, u32[]{:S(2)}) copy-start(bf16[1,4096,256]{2,1,0:T(8,128)(2,1)} %param.12) | copy-start | bytes 6291460
  21.2 14.1 %copy-start.1 = (bf16[1,256,7680]{2,1,0:T(8,128)(2,1)S(1)}, bf16[1,256,7680]{2,1,0:T(8,128)(2,1)}, u32[]{:S(2)}) copy-start(bf16[1,256,7680]{2,1,0:T(8,128)(2,1)} %param.13) | copy-start | bytes 11796484
  40.0 32.3 %collective-permute-start = (f32[16,7680]{1,0:T(8,128)}, f32[16,7680]{1,0:T(8,128)}, u32[]{:S(2)}, u32[]{:S(2)}) collective-permute-start(f32[16,7680]{1,0:T(8,128)} %get-tuple-element.40), channel_id=1, source_target_pairs={{0,8},{8,16},{16,24},{24,0},{1,9},{9,17},{17,25},{25,1},{2,10},{10... | collective-permute-start | bytes 1474568 | tf_op jit(solution)/shard_map/ppermute | solution.py:216
  41.5 30.9 %collective-permute-start.1 = (f32[16,7680]{1,0:T(8,128)}, f32[16,7680]{1,0:T(8,128)}, u32[]{:S(2)}, u32[]{:S(2)}) collective-permute-start(f32[16,7680]{1,0:T(8,128)} %get-tuple-element.39), channel_id=1, source_target_pairs={{0,16},{8,24},{16,0},{24,8},{1,17},{9,25},{17,1},{25,9},{2,18},{10... | collective-permute-start | bytes 1474568 | tf_op jit(solution)/shard_map/ppermute | solution.py:216
  42.9 29.5 %collective-permute-start.2 = (f32[16,7680]{1,0:T(8,128)}, f32[16,7680]{1,0:T(8,128)}, u32[]{:S(2)}, u32[]{:S(2)}) collective-permute-start(f32[16,7680]{1,0:T(8,128)} %get-tuple-element.38), channel_id=1, source_target_pairs={{0,24},{8,0},{16,8},{24,16},{1,25},{9,1},{17,9},{25,17},{2,26},{10... | collective-permute-start | bytes 1474568 | tf_op jit(solution)/shard_map/ppermute | solution.py:216
  45.7 6.0 %copy-start.6 = (bf16[4096,1]{0,1:T(2,128)(2,1)S(1)}, bf16[4096,1]{0,1:T(2,128)(2,1)}, u32[]{:S(2)}) copy-start(bf16[4096,1]{0,1:T(2,128)(2,1)} %param.11) | copy-start | bytes 24580
  65.1 9.2 %copy-start.7 = (f32[16]{0:T(128)S(1)}, f32[16]{0:T(128)}, u32[]{:S(2)}) copy-start(f32[16]{0:T(128)} %select_reduce_fusion.1) | copy-start | bytes 196
  72.3 18.2 %copy-start.2 = (bf16[1,256,7680]{2,1,0:T(8,128)(2,1)S(1)}, bf16[1,256,7680]{2,1,0:T(8,128)(2,1)}, u32[]{:S(2)}) copy-start(bf16[1,256,7680]{2,1,0:T(8,128)(2,1)} %param.13) | copy-start | bytes 11796484
  90.5 2.6 %copy-start.3 = (bf16[4,16,7680]{2,1,0:T(8,128)(2,1)S(1)}, bf16[4,16,7680]{2,1,0:T(8,128)(2,1)}, u32[]{:S(2)}) copy-start(bf16[4,16,7680]{2,1,0:T(8,128)(2,1)} %shard_map.113) | copy-start | bytes 2949124
  93.2 8.3 %copy-start.4 = (bf16[4,16,4096]{2,1,0:T(8,128)(2,1)S(1)}, bf16[4,16,4096]{2,1,0:T(8,128)(2,1)}, u32[]{:S(2)}) copy-start(bf16[4,16,4096]{2,1,0:T(8,128)(2,1)} %shard_map.111) | copy-start | bytes 1572868
  97.1 7.1 %collective-permute-start.3 = (bf16[16,4096]{1,0:T(8,128)(2,1)S(1)}, bf16[16,4096]{1,0:T(8,128)(2,1)S(1)}, u32[]{:S(2)}, u32[]{:S(2)}) collective-permute-start(bf16[16,4096]{1,0:T(8,128)(2,1)S(1)} %get-tuple-element.42), channel_id=1, source_target_pairs={{0,8},{8,16},{16,24},{24,0},{1,9},{9,17},{17,25},{25,1},{2,10},{10... | collective-permute-start | bytes 393224 | tf_op jit(solution)/shard_map/ppermute | solution.py:216
  98.5 7.0 %collective-permute-start.4 = (bf16[16,4096]{1,0:T(8,128)(2,1)S(1)}, bf16[16,4096]{1,0:T(8,128)(2,1)S(1)}, u32[]{:S(2)}, u32[]{:S(2)}) collective-permute-start(bf16[16,4096]{1,0:T(8,128)(2,1)S(1)} %get-tuple-element.44), channel_id=1, source_target_pairs={{0,16},{8,24},{16,0},{24,8},{1,17},{9,25},{17,1},{25,9},{2,18},{10... | collective-permute-start | bytes 393224 | tf_op jit(solution)/shard_map/ppermute | solution.py:216
  99.1 6.4 %collective-permute-start.5 = (bf16[16,4096]{1,0:T(8,128)(2,1)S(1)}, bf16[16,4096]{1,0:T(8,128)(2,1)S(1)}, u32[]{:S(2)}, u32[]{:S(2)}) collective-permute-start(bf16[16,4096]{1,0:T(8,128)(2,1)S(1)} %get-tuple-element.43), channel_id=1, source_target_pairs={{0,24},{8,0},{16,8},{24,16},{1,25},{9,1},{17,9},{25,17},{2,26},{10... | collective-permute-start | bytes 393224 | tf_op jit(solution)/shard_map/ppermute | solution.py:216
  126.6 5.6 %copy-start.5 = (f32[16,2048]{1,0:T(8,128)S(1)}, f32[16,2048]{1,0:T(8,128)}, u32[]{:S(2)}) copy-start(f32[16,2048]{1,0:T(8,128)} %get-tuple-element.28) | copy-start | bytes 393220

commit v5 on v4

--- a/solution.py
+++ b/solution.py
@@ -131,7 +131,7 @@
 
 
 def pair_scatter_body(
-    axis, n, other, m, x, whole, parts, out, wholes, gathered,
+    axis, n, other, m, x, whole, out, wholes,
     theirs, leaving, landed, send, recv, pair_send, pair_recv, far_send, far_recv, local,
 ):
     here = lax.axis_index(other)
@@ -151,11 +151,9 @@
     for k, peer in enumerate(far):
         crossing += [
             remote(whole, wholes.at[here], far_send.at[0, k], far_recv.at[0, k], other, peer),
-            remote(parts.at[peer], gathered.at[here], far_send.at[1, k], far_recv.at[1, k], other, peer),
         ]
     crossing += [
         pltpu.make_async_copy(whole, wholes.at[here], local.at[0]),
-        pltpu.make_async_copy(parts.at[here], gathered.at[here], local.at[1]),
     ]
     for copy in crossing:
         copy.start()
@@ -177,25 +175,24 @@
         copy.wait()
 
 
-def pair_scatter(axis, x, other, whole, parts, collective_id):
+def pair_scatter(axis, x, other, whole, collective_id):
     n, m = lax.axis_size(axis), lax.axis_size(other)
     half = n // 2
     block = x.shape[1:]
     dma = pltpu.SemaphoreType.DMA
     return call(
         functools.partial(pair_scatter_body, axis, n, other, m),
-        [x, whole, parts],
+        [x, whole],
         [
             jax.ShapeDtypeStruct(block, x.dtype),
             jax.ShapeDtypeStruct((m, *whole.shape), whole.dtype),
-            jax.ShapeDtypeStruct(parts.shape, parts.dtype),
         ],
         [
             pltpu.VMEM((half, *block), x.dtype),
             pltpu.VMEM((half - 1, *block), jnp.bfloat16),
             pltpu.VMEM((half - 1, *block), jnp.bfloat16),
             dma((half - 1,)), dma((half - 1,)), dma((half,)), dma((half,)),
-            dma((2, m - 1)), dma((2, m - 1)), dma((2,)),
+            dma((1, m - 1)), dma((1, m - 1)), dma((1,)),
         ],
         collective_id,
     )
@@ -247,7 +244,8 @@
     own_words = jnp.sum(jnp.where(own_select, offset[None, :] % CV, 0), axis=1).astype(jnp.int32)
     own_gains = jnp.sum(jnp.where(own_select, gain_rows[None, :], 0.0), axis=1)
     own_rows = jnp.dot(own_select.astype(bf16), rows_hidden, preferred_element_type=f32).astype(bf16)
-    (tail_rows,) = exchange("dp", [own_rows], [], 2)
+    pieces = rows_hidden.reshape(span, n_dp, share).transpose(1, 0, 2)
+    tail_rows, hidden_columns = exchange("dp", [own_rows], [pieces], 2)
     tail_rows = tail_rows.reshape(n_dp * cap, model)
 
     proj = tail_proj[0]
@@ -285,7 +283,6 @@
     deltas = jnp.concatenate([head_delta, cluster_delta], axis=1)
     deltas = jnp.pad(deltas, ((0, 0), (0, -deltas.shape[1] % 128)))
     deltas, token_partial, logit_parts = lax.optimization_barrier((deltas, token_partial, logit_parts))
-    pieces = rows_hidden.reshape(span, n_dp, share).transpose(1, 0, 2)
 
     word_logits = functools.reduce(jnp.add, logit_parts)
     word_top = jnp.max(word_logits, axis=1, keepdims=True)
@@ -315,7 +312,7 @@
         own_select.astype(bf16), tail_sum, (((0,), (0,)), ((), ())), preferred_element_type=f32
     )
     partial = (token_partial + spread_back).reshape(n_vocab, 2 * local, model // 2)
-    hidden_grad, deltas, hidden_columns = pair_scatter("vocab", partial, "dp", deltas, pieces, 6)
+    hidden_grad, deltas = pair_scatter("vocab", partial, "dp", deltas, 6)
     hidden_grad = hidden_grad.reshape(local, model).astype(bf16)
     deltas = deltas.reshape(n_dp * span, -1)
     hidden_columns = hidden_columns.reshape(n_dp * span, share)

time: 134 us -> 132 us (0.985)
  other arithmetic: 10.7 us -> 7.91 us
  local copies, waits for them, and re-layouts: 10.7 us -> 12.1 us
    another operation x0 -> x2, local copies, waits for them, and re-layouts: none -> 2.34 us  [shards(): pieces = rows_hidden.reshape(span, n_dp, share).transpose(1, 0, 2)]
  transfers between devices with their start and end apart: 6 -> 6, of which waited for: 2 -> 2; matrix products, arithmetic and copies ran while one was open for 17% -> 15% of each run, Pallas kernels for 5% -> 5%
where the time goes in v5:
time: 132 us; the launch traced here: 131 us
  Pallas kernels  67.7 us (51%)
  matrix products  31.7 us (24%)
  local copies, waits for them, and re-layouts  12.1 us (9%)
  starting transfers between devices  8.67 us (7%)
  other arithmetic  7.91 us (6%)
  waiting for transfers between devices  2.03 us (2%)
    pallas_call x5, Pallas kernels, call(): pl.pallas_call(body, out_shape=results, in_specs=[vmem] * len(operands),...  67.7 us
    ppermute x6, starting transfers between devices, scatter_turned(): lax.ppermute(part(k), axis, turned(axis, k))  8.67 us
    dot_general x1, matrix products, shards(): lax.dot_general(head_delta, head_weight, (((1,), (1,)), ((), ())), prefer...  7.23 us
    dot_general x1, matrix products, shards(): local_logits = jnp.dot(rows_hidden, head_weight, preferred_element_type=f32)  6 us
    dot_general x1, matrix products, shards(): lax.dot_general(hidden_columns, all_delta, (((0,), (0,)), ((), ())), pref...  3.65 us
    dot_general x1, matrix products, shards(): lax.dot_general(reduced, word_delta, (((0,), (0,)), ((), ())), preferred_...  3.13 us
  transfers between devices with their start and end apart: 6, of which 2 were waited for; matrix products, arithmetic and copies ran while one was open for 15% of the time, Pallas kernels for 5%

profile of v5, /device:TPU:0, one launch (start us, length us, event | category | flops | bytes accessed | tf_op | source)
XLA Modules:
  0.0 131.1 jit_solution(14545258652324040637)
XLA Ops:
  0.7 1.6 %reshape.116.refs_0_ = bf16[16,2048]{1,0:T(8,128)(2,1)} reshape(bf16[8,4096]{1,0:T(8,128)(2,1)} %param.7) | data formatting | bytes 131072 | tf_op jit(solution)/shard_map/reshape | solution.py:232
  4.2 14.8 %shard_map.110 = (bf16[8,16,2048]{2,1,0:T(8,128)(2,1)}, f32[8,8,128]{2,1,0:T(8,128)}) custom-call(bf16[16,2048]{1,0:T(8,128)(2,1)} %reshape.116.refs_0_, f32[8,128]{1,0:T(8,128)} %select_maximum_fusion.1.refs_1_), custom_call_target="tpu_custom_call" | custom-call | tf_op jit(solution)/shard_map/pallas_call | solution.py:34
  19.0 1.2 reshape.117
  20.2 1.4 %reshape_reshape.3 = bf16[64,4,1024]{2,1,0:T(4,128)(2,1)S(1)} reshape(bf16[8,16,2048]{2,1,0:T(8,128)(2,1)} %get-tuple-element.20) | data formatting | bytes 1048576 | tf_op jit(solution)/shard_map/reshape;reshape | solution.py:247
  21.6 0.8 convert_reduce_fusion.1
  22.6 1.0 copy.25
  23.6 0.8 convolution_convert_fusion.3.refs_0_
  24.4 17.5 %shard_map.111 = (bf16[4,16,4096]{2,1,0:T(8,128)(2,1)}, bf16[4,64,1024]{2,1,0:T(8,128)(2,1)}) custom-call(bf16[16,4096]{1,0:T(8,128)(2,1)} %convolution_convert_fusion.3.refs_0_, bf16[4,64,1024]{2,1,0:T(8,128)(2,1)} %bitcast.62), custom_call_target="tpu_custom_call" | custom-call | tf_op jit(solution)/shard_map/pallas_call | solution.py:34
  41.9 1.5 %fusion.12 = bf16[64,256]{1,0:T(8,128)(2,1)S(1)} fusion(bf16[64,4096]{1,0:T(8,128)(2,1)} %bitcast.63, bf16[1,4096,256]{2,1,0:T(8,128)(2,1)S(1)} %copy-done), kind=kOutput, calls=%fused_computation.16 | convolution fusion | flops 134234112 | bytes 2654208 | tf_op jit(solution)/shard_map/dot_general | solution.py:253
  43.4 2.1 %fusion.4 = f32[64,7680]{1,0:T(8,128)} fusion(bf16[64,256]{1,0:T(8,128)(2,1)S(1)} %fusion.12, bf16[1,256,7680]{2,1,0:T(8,128)(2,1)S(1)} %copy-done.1), kind=kOutput, calls=%fused_computation.9 | convolution fusion | flops 251658240 | bytes 5931008 | tf_op jit(solution)/shard_map/dot_general | solution.py:254
  45.5 2.6 %constant_dynamic-slice_fusion.3 = (f32[16,7680]{1,0:T(8,128)}, f32[16,7680]{1,0:T(8,128)}, f32[16,7680]{1,0:T(8,128)}, f32[16,7680]{1,0:T(8,128)S(1)}) fusion(f32[64,7680]{1,0:T(8,128)} %fusion.4, s32[]{:T(128)S(6)} %select_n.62, s32[]{:T(128)S(6)} %select_n.61, s32[]{:T(128)S(6)} %select_n.60, s32[]{:T(128)S(6)} %select_n.59), kind=kLoop, calls=%fused_computation.60 | loop fusion | bytes 3932176 | tf_op jit(solution)/shard_map/dynamic_slice | solution.py:211
  48.1 1.4 %collective-permute-start = (f32[16,7680]{1,0:T(8,128)}, f32[16,7680]{1,0:T(8,128)}, u32[]{:S(2)}, u32[]{:S(2)}) collective-permute-start(f32[16,7680]{1,0:T(8,128)} %get-tuple-element.42), channel_id=1, source_target_pairs={{0,8},{8,16},{16,24},{24,0},{1,9},{9,17},{17,25},{25,1},{2,10},{10... | collective-permute-start | bytes 1474568 | tf_op jit(solution)/shard_map/ppermute | solution.py:213
  49.5 1.5 %collective-permute-start.1 = (f32[16,7680]{1,0:T(8,128)}, f32[16,7680]{1,0:T(8,128)}, u32[]{:S(2)}, u32[]{:S(2)}) collective-permute-start(f32[16,7680]{1,0:T(8,128)} %get-tuple-element.41), channel_id=1, source_target_pairs={{0,16},{8,24},{16,0},{24,8},{1,17},{9,25},{17,1},{25,9},{2,18},{10... | collective-permute-start | bytes 1474568 | tf_op jit(solution)/shard_map/ppermute | solution.py:213
  51.0 1.4 %collective-permute-start.2 = (f32[16,7680]{1,0:T(8,128)}, f32[16,7680]{1,0:T(8,128)}, u32[]{:S(2)}, u32[]{:S(2)}) collective-permute-start(f32[16,7680]{1,0:T(8,128)} %get-tuple-element.40), channel_id=1, source_target_pairs={{0,24},{8,0},{16,8},{24,16},{1,25},{9,1},{17,9},{25,17},{2,26},{10... | collective-permute-start | bytes 1474568 | tf_op jit(solution)/shard_map/ppermute | solution.py:213
  52.4 0.8 slice_reduce_fusion
  53.2 6.0 %fusion.39 = (f32[64]{0:T(128)S(1)}, f32[64,1280]{1,0:T(8,128)S(1)}) fusion(bf16[64,4096]{1,0:T(8,128)(2,1)S(1)} %reshape.117, bf16[4096,1280]{1,0:T(8,128)(2,1)} %param.10), kind=kOutput, calls=%fused_computation.80 | convolution fusion | flops 671170496 | bytes 11337984 | tf_op jit(solution)/shard_map/dot_general | solution.py:259
  60.3 6.8 %shard_map.112 = f32[8,8,128]{2,1,0:T(8,128)} custom-call(f32[8,128]{1,0:T(8,128)} %select_maximum_fusion.refs_0_), custom_call_target="tpu_custom_call" | custom-call | tf_op jit(solution)/shard_map/pallas_call | solution.py:34
  67.2 0.8 fusion.38
  69.5 7.2 %convolution_add_fusion = f32[64,4096]{1,0:T(8,128)S(1)} fusion(bf16[64,1280]{1,0:T(8,128)(2,1)S(1)} %multiply_convert_fusion.1, bf16[4096,1280]{1,0:T(8,128)(2,1)} %param.10, f32[4096]{0:T(1024)S(1)} %mul.67, f32[64]{0:T(128)S(1)} %get-tuple-element.35), kind=kOutput, calls=%fused_computation.4 | convolution fusion | flops 671612928 | bytes 11714816 | tf_op jit(solution)/shard_map/dot_general | solution.py:279
  76.7 1.7 %fusion.35 = (f32[16]{0:T(128)S(1)}, f32[16,7680]{1,0:T(8,128)S(1)}) fusion(f32[16,7680]{1,0:T(8,128)} %collective-permute-done.2, f32[16,7680]{1,0:T(8,128)} %collective-permute-done.1, f32[16,7680]{1,0:T(8,128)S(1)} %get-tuple-element.25, f32[16,7680]{1,0:T(8,128)} %collective-permute-done), kind=kLoop, calls=%fused_computation.77 | loop fusion | flops 491504 | bytes 2457664 | tf_op jit(solution)/shard_map/reduce_max | solution.py:288
  78.7 0.9 multiply_convert_fusion.refs_0_
  79.6 15.3 %shard_map.113 = bf16[4,16,7680]{2,1,0:T(8,128)(2,1)} custom-call(bf16[16,7680]{1,0:T(8,128)(2,1)} %multiply_convert_fusion.refs_0_), custom_call_target="tpu_custom_call" | custom-call | tf_op jit(solution)/shard_map/pallas_call | solution.py:34
  95.0 2.6 %fusion.9 = bf16[64,256]{1,0:T(8,128)(2,1)S(1)} fusion(bf16[64,7680]{1,0:T(8,128)(2,1)} %bitcast.60, bf16[1,256,7680]{2,1,0:T(8,128)(2,1)S(1)} %copy-done.2), kind=kOutput, calls=%fused_computation.15 | convolution fusion | flops 251674624 | bytes 4947968 | tf_op jit(solution)/shard_map/dot_general | solution.py:296
  97.6 3.1 %fusion = bf16[1,256,7680]{2,1,0:T(8,128)(2,1)} fusion(bf16[64,256]{1,0:T(8,128)(2,1)S(1)} %fusion.12, bf16[64,7680]{1,0:T(8,128)(2,1)S(1)} %bitcast.61), kind=kOutput, calls=%fused_computation.1 | convolution fusion | flops 253624320 | bytes 4947968 | tf_op jit(solution)/shard_map/dot_general | solution.py:304
  101.5 1.4 %collective-permute-start.3 = (bf16[16,4096]{1,0:T(8,128)(2,1)S(1)}, bf16[16,4096]{1,0:T(8,128)(2,1)S(1)}, u32[]{:S(2)}, u32[]{:S(2)}) collective-permute-start(bf16[16,4096]{1,0:T(8,128)(2,1)S(1)} %get-tuple-element.44), channel_id=1, source_target_pairs={{0,8},{8,16},{16,24},{24,0},{1,9},{9,17},{17,25},{25,1},{2,10},{10... | collective-permute-start | bytes 393224 | tf_op jit(solution)/shard_map/ppermute | solution.py:213
  103.5 2.3 %collective-permute-start.5 = (bf16[16,4096]{1,0:T(8,128)(2,1)S(1)}, bf16[16,4096]{1,0:T(8,128)(2,1)S(1)}, u32[]{:S(2)}, u32[]{:S(2)}) collective-permute-start(bf16[16,4096]{1,0:T(8,128)(2,1)S(1)} %get-tuple-element.45), channel_id=1, source_target_pairs={{0,24},{8,0},{16,8},{24,16},{1,25},{9,1},{17,9},{25,17},{2,26},{10... | collective-permute-start | bytes 393224 | tf_op jit(solution)/shard_map/ppermute | solution.py:213
  105.9 2.1 %fusion.1 = bf16[1,4096,256]{2,1,0:T(8,128)(2,1)} fusion(bf16[64,4096]{1,0:T(8,128)(2,1)S(1)} %bitcast.64, bf16[64,256]{1,0:T(8,128)(2,1)S(1)} %fusion.9), kind=kOutput, calls=%fused_computation.3 | convolution fusion | flops 135266304 | bytes 2654208 | tf_op jit(solution)/shard_map/dot_general | solution.py:307
  108.6 1.4 %collective-permute-done.4 = bf16[16,4096]{1,0:T(8,128)(2,1)S(1)} collective-permute-done((bf16[16,4096]{1,0:T(8,128)(2,1)S(1)}, bf16[16,4096]{1,0:T(8,128)(2,1)S(1)}, u32[]{:S(2)}, u32[]{:S(2)}) %collective-permute-start.4) | collective-permute-done | bytes 131104 | tf_op jit(solution)/shard_map/ppermute | solution.py:213
  110.4 1.1 reshape.121.x
  111.5 13.3 %shard_map.114 = (f32[16,2048]{1,0:T(8,128)}, bf16[4,64,1408]{2,1,0:T(8,128)(2,1)}) custom-call(f32[8,16,2048]{2,1,0:T(8,128)} %reshape.121.x, bf16[64,1408]{1,0:T(8,128)(2,1)} %fusion.19.whole), custom_call_target="tpu_custom_call" | custom-call | tf_op jit(solution)/shard_map/pallas_call | solution.py:34
  124.9 1.3 fusion.22
  126.2 3.6 %convolution_convert_fusion.4 = bf16[1024,1280]{1,0:T(8,128)(2,1)} fusion(bf16[256,1024]{1,0:T(8,128)(2,1)} %bitcast.66, bf16[256,1408]{1,0:T(8,128)(2,1)} %bitcast.68), kind=kOutput, calls=%fused_computation.11 | convolution fusion | flops 672399360 | bytes 3801088 | tf_op jit(solution)/shard_map/dot_general | solution.py:321
  (52 shorter events, 8.7 us)
Async XLA Ops:
  0.6 41.3 %copy-start = (bf16[1,4096,256]{2,1,0:T(8,128)(2,1)S(1)}, bf16[1,4096,256]{2,1,0:T(8,128)(2,1)}, u32[]{:S(2)}) copy-start(bf16[1,4096,256]{2,1,0:T(8,128)(2,1)} %param.12) | copy-start | bytes 6291460
  22.5 20.9 %copy-start.1 = (bf16[1,256,7680]{2,1,0:T(8,128)(2,1)S(1)}, bf16[1,256,7680]{2,1,0:T(8,128)(2,1)}, u32[]{:S(2)}) copy-start(bf16[1,256,7680]{2,1,0:T(8,128)(2,1)} %param.13) | copy-start | bytes 11796484
  48.1 28.6 %collective-permute-start = (f32[16,7680]{1,0:T(8,128)}, f32[16,7680]{1,0:T(8,128)}, u32[]{:S(2)}, u32[]{:S(2)}) collective-permute-start(f32[16,7680]{1,0:T(8,128)} %get-tuple-element.42), channel_id=1, source_target_pairs={{0,8},{8,16},{16,24},{24,0},{1,9},{9,17},{17,25},{25,1},{2,10},{10... | collective-permute-start | bytes 1474568 | tf_op jit(solution)/shard_map/ppermute | solution.py:213
  49.5 27.2 %collective-permute-start.1 = (f32[16,7680]{1,0:T(8,128)}, f32[16,7680]{1,0:T(8,128)}, u32[]{:S(2)}, u32[]{:S(2)}) collective-permute-start(f32[16,7680]{1,0:T(8,128)} %get-tuple-element.41), channel_id=1, source_target_pairs={{0,16},{8,24},{16,0},{24,8},{1,17},{9,25},{17,1},{25,9},{2,18},{10... | collective-permute-start | bytes 1474568 | tf_op jit(solution)/shard_map/ppermute | solution.py:213
  51.0 25.7 %collective-permute-start.2 = (f32[16,7680]{1,0:T(8,128)}, f32[16,7680]{1,0:T(8,128)}, u32[]{:S(2)}, u32[]{:S(2)}) collective-permute-start(f32[16,7680]{1,0:T(8,128)} %get-tuple-element.40), channel_id=1, source_target_pairs={{0,24},{8,0},{16,8},{24,16},{1,25},{9,1},{17,9},{25,17},{2,26},{10... | collective-permute-start | bytes 1474568 | tf_op jit(solution)/shard_map/ppermute | solution.py:213
  53.2 6.0 %copy-start.6 = (bf16[4096,1]{0,1:T(2,128)(2,1)S(1)}, bf16[4096,1]{0,1:T(2,128)(2,1)}, u32[]{:S(2)}) copy-start(bf16[4096,1]{0,1:T(2,128)(2,1)} %param.11) | copy-start | bytes 24580
  76.7 18.3 %copy-start.2 = (bf16[1,256,7680]{2,1,0:T(8,128)(2,1)S(1)}, bf16[1,256,7680]{2,1,0:T(8,128)(2,1)}, u32[]{:S(2)}) copy-start(bf16[1,256,7680]{2,1,0:T(8,128)(2,1)} %param.13) | copy-start | bytes 11796484
  94.9 2.6 %copy-start.3 = (bf16[4,16,7680]{2,1,0:T(8,128)(2,1)S(1)}, bf16[4,16,7680]{2,1,0:T(8,128)(2,1)}, u32[]{:S(2)}) copy-start(bf16[4,16,7680]{2,1,0:T(8,128)(2,1)} %shard_map.113) | copy-start | bytes 2949124
  97.6 8.3 %copy-start.4 = (bf16[4,16,4096]{2,1,0:T(8,128)(2,1)S(1)}, bf16[4,16,4096]{2,1,0:T(8,128)(2,1)}, u32[]{:S(2)}) copy-start(bf16[4,16,4096]{2,1,0:T(8,128)(2,1)} %get-tuple-element.21) | copy-start | bytes 1572868
  101.5 7.1 %collective-permute-start.3 = (bf16[16,4096]{1,0:T(8,128)(2,1)S(1)}, bf16[16,4096]{1,0:T(8,128)(2,1)S(1)}, u32[]{:S(2)}, u32[]{:S(2)}) collective-permute-start(bf16[16,4096]{1,0:T(8,128)(2,1)S(1)} %get-tuple-element.44), channel_id=1, source_target_pairs={{0,8},{8,16},{16,24},{24,0},{1,9},{9,17},{17,25},{25,1},{2,10},{10... | collective-permute-start | bytes 393224 | tf_op jit(solution)/shard_map/ppermute | solution.py:213
  102.9 7.0 %collective-permute-start.4 = (bf16[16,4096]{1,0:T(8,128)(2,1)S(1)}, bf16[16,4096]{1,0:T(8,128)(2,1)S(1)}, u32[]{:S(2)}, u32[]{:S(2)}) collective-permute-start(bf16[16,4096]{1,0:T(8,128)(2,1)S(1)} %get-tuple-element.46), channel_id=1, source_target_pairs={{0,16},{8,24},{16,0},{24,8},{1,17},{9,25},{17,1},{25,9},{2,18},{10... | collective-permute-start | bytes 393224 | tf_op jit(solution)/shard_map/ppermute | solution.py:213
  103.5 6.4 %collective-permute-start.5 = (bf16[16,4096]{1,0:T(8,128)(2,1)S(1)}, bf16[16,4096]{1,0:T(8,128)(2,1)S(1)}, u32[]{:S(2)}, u32[]{:S(2)}) collective-permute-start(bf16[16,4096]{1,0:T(8,128)(2,1)S(1)} %get-tuple-element.45), channel_id=1, source_target_pairs={{0,24},{8,0},{16,8},{24,16},{1,25},{9,1},{17,9},{25,17},{2,26},{10... | collective-permute-start | bytes 393224 | tf_op jit(solution)/shard_map/ppermute | solution.py:213
  124.9 5.6 %copy-start.5 = (f32[16,2048]{1,0:T(8,128)S(1)}, f32[16,2048]{1,0:T(8,128)}, u32[]{:S(2)}) copy-start(f32[16,2048]{1,0:T(8,128)} %get-tuple-element.30) | copy-start | bytes 393220
